TPU v7x, 256 devices: a whole 4x4x8 slice. The times are simulated.
256 devices in a mesh: batch: 16 (over z, core), tensor: 16 (over y, x).
Axes of the slice: x: 4, y: 4, z: 8, core: 2. Of those that a mesh axis runs over, the one named last changes fastest.
Arguments:
- inputs: bfloat16 [3, 256, 8192], P(None, None, 'batch'), may hold values from -40 to 40
- in_gain: float32 [8192], P('batch'), may hold values from 0.1 to 1.9
- qkv_weight: bfloat16 [8192, 24576], P('batch', 'tensor'), may hold values from -0.0625 to 0.0625
- decay: float32 [64], P('tensor'), may hold values from 0.25 to 0.99
- state: float32 [256, 64, 128, 128], P('batch', 'tensor'), may hold values from -1.8 to 1.8
- head_gain: float32 [8192], P('tensor'), may hold values from 0.1 to 1.9
- out_weight: bfloat16 [8192, 8192], P('tensor', 'batch'), may hold values from -0.0625 to 0.0625
- mid_gain: float32 [8192], P('batch'), may hold values from 0.1 to 1.9
- up_weight: bfloat16 [8192, 28672], P('batch', 'tensor'), may hold values from -0.0625 to 0.0625
- down_weight: bfloat16 [28672, 8192], P('tensor', 'batch'), may hold values from -0.03125 to 0.03125
- att_mask: int32 [3, 256, 8192], P(None, 'batch', 'tensor'), may hold values 0 or 1
- ffn_mask: int32 [3, 256, 28672], P(None, 'batch', 'tensor'), may hold values 0 or 1
Outputs:
- outputs: bfloat16 [3, 256, 8192], P(None, 'tensor', 'batch')
All inputs are finite; a program needn't handle non-finite values. No bound on the sum of `att_mask` or of `ffn_mask` on one device may be relied on, other than what follows from the above.
Results may differ from a plain program's by a relative error of at most 0.0038.
Values may be sent and summed in bfloat16 or wider, within the bound.
No kernel may reach another device: no remote copies, remote signals or barrier semaphores. Data moves between devices by JAX's collectives and lax.ppermute only.
A program may use at most 64 MiB of HBM per device.

v0:
```python
import functools

import jax
import jax.numpy as jnp
from jax import lax
from jax.experimental import pallas as pl
from jax.experimental.pallas import tpu as pltpu
from jax.sharding import Mesh
from jax.sharding import PartitionSpec as P

D = 8192
STEPS = 3
DH = 128
EPS = 1e-06
LANES = 128
CHAINS = 2
GATHER_CHAINS = 2
BATCH = ("z", "core")
TENSOR = ("y", "x")
VMEM = pltpu.CompilerParams(vmem_limit_bytes=14 * 1024 * 1024)


def edges_of(width, count):
    tiles = width // LANES
    cuts = [LANES * (tiles * i // count) for i in range(count + 1)]
    return list(zip(cuts[:-1], cuts[1:], strict=True))


def swap_cores(value):
    return lax.ppermute(value, "core", [(0, 1), (1, 0)])


def pass_on(value):
    zs = lax.axis_size("z")
    pairs = []
    for z in range(zs):
        pairs.append((2 * z, 2 * ((z + 1) % zs)))
        pairs.append((2 * z + 1, 2 * ((z - 1) % zs) + 1))
    return lax.ppermute(value, BATCH, pairs)


def pieces_of(sums, source):
    high = lax.reduce_precision(sums, 8, 7)
    middle = lax.reduce_precision(sums - high, 8, 7)
    low = sums - high - middle
    lane = lax.broadcasted_iota(jnp.int32, (sums.shape[0], LANES), 1) - 3 * source
    return jnp.where(lane == 0, high, jnp.where(lane == 1, middle, jnp.where(lane == 2, low, 0.0)))


def product_kernel(chips, first, which, place_ref, rows_ref, gain_ref, weight_ref, out_ref, picked_ref):
    width = weight_ref.shape[1]
    share = picked_ref.shape[0] // (2 * STEPS * chips)
    zs = rows_ref.shape[1] // (2 * share) if first else rows_ref.shape[0] // 2
    start, source = place_ref[which], place_ref[2]
    gain = gain_ref[...] if first else 1.0 / gain_ref[...]
    for c in range(chips):
        chip = start + c
        chip = jnp.where(chip >= zs, chip - zs, chip)
        for core in range(2):
            for step in range(STEPS):
                at = ((c * 2 + core) * STEPS + step) * share
                if first:
                    from_row = pl.multiple_of(chip * (2 * share) + core * share, share)
                    values = rows_ref[step, pl.ds(from_row, share), :].astype(jnp.float32)
                    picked_ref[at : at + share, :] = (values * gain).astype(jnp.bfloat16)
                else:
                    block = rows_ref[chip * 2 + core, step * share : (step + 1) * share, :]
                    picked_ref[at : at + share, :] = block
                    values = block.astype(jnp.float32) * gain
                squares = jnp.sum(values * values, axis=-1, keepdims=True)
                out_ref[at : at + share, width:] = pieces_of(squares, source).astype(out_ref.dtype)
    chunk = 256
    for at in range(0, width, chunk):
        out_ref[:, at : at + chunk] = jnp.dot(
            picked_ref[...], weight_ref[:, at : at + chunk], preferred_element_type=jnp.float32
        ).astype(out_ref.dtype)


def product(rows, gain, weight, chips, which, place, first):
    share = (rows.shape[1] // 16) if first else rows.shape[1] // STEPS
    count = chips * 2 * STEPS * share
    depth, width = weight.shape
    if first:
        rows = pltpu.with_memory_space_constraint(rows, pltpu.HBM)
        weight = pltpu.with_memory_space_constraint(weight, pltpu.HBM)
    out = pl.pallas_call(
        functools.partial(product_kernel, chips, first, which),
        in_specs=[pl.BlockSpec(memory_space=pltpu.SMEM)] + [pl.BlockSpec(memory_space=pltpu.VMEM)] * 3,
        out_specs=pl.BlockSpec(memory_space=pltpu.VMEM),
        out_shape=jax.ShapeDtypeStruct((count, width + LANES), jnp.bfloat16),
        scratch_shapes=[pltpu.VMEM((count, depth), jnp.bfloat16)],
        compiler_params=VMEM,
    )(place, rows, gain[None, :], weight)
    return out.reshape(chips, 2, STEPS * share, width + LANES)


def sum_to_owner(rows, gain, weight, place, ahead, first):
    half = lax.axis_size("z") // 2
    theirs = product(rows, gain, weight, half, 0, place, first)
    got = swap_cores(theirs)
    mine = product(rows, gain, weight, half + 1, 1, place, first)

    def at(distance):
        own = jnp.where(ahead, mine[distance], mine[half - distance]).astype(jnp.float32)
        other = jnp.where(ahead, got[distance - 1], got[half - distance]).astype(jnp.float32)
        return own + other

    width = mine.shape[-1]
    edges = edges_of(width, CHAINS)
    which = (lax.broadcasted_iota(jnp.int32, (2, 1, 1), 0) == 0) == ahead
    farthest = at(half)
    carried = jnp.where(ahead, farthest[0], farthest[1]).astype(jnp.bfloat16)
    carried = [pass_on(carried[:, low:high]) for low, high in edges]
    parts = at(half - 1)
    totals = [
        parts[..., low:high] + jnp.where(which, part.astype(jnp.float32)[None], 0.0)
        for (low, high), part in zip(edges, carried, strict=True)
    ]
    for distance in range(half - 2, -1, -1):
        carried = [pass_on(total.astype(jnp.bfloat16)).astype(jnp.float32) for total in totals]
        parts = at(distance) if distance > 0 else jnp.where(ahead, mine[0], mine[half]).astype(jnp.float32)
        totals = [parts[..., low:high] + part for (low, high), part in zip(edges, carried, strict=True)]
    away = [swap_cores(jnp.where(ahead, total[1], total[0]).astype(jnp.bfloat16)) for total in totals]
    ours = [jnp.where(ahead, total[0], total[1]) for total in totals]
    return jnp.concatenate(ours, axis=-1), jnp.concatenate(away, axis=-1)


def attention_kernel(decay_ref, ours_ref, our_sums_ref, theirs_ref, their_sums_ref, state_ref, gain_ref, mask_ref, out_ref):
    head = pl.program_id(0)
    rows = ours_ref.shape[0]
    mine = rows // STEPS
    squares = jnp.sum(our_sums_ref[...] + their_sums_ref[...].astype(jnp.float32), axis=-1, keepdims=True)
    parts = (ours_ref[...] + theirs_ref[...].astype(jnp.float32)) * lax.rsqrt(squares / D + EPS)
    scale = DH ** (-0.5)
    queries = parts[:, :DH] * scale
    keys = parts[:, DH : 2 * DH] * scale
    values = parts[:, 2 * DH :]
    rate = decay_ref[head]
    turned = queries.T
    found = [[] for _ in range(STEPS)]
    for request in range(mine):
        block = state_ref[request, 0]
        for step in range(STEPS):
            at = step * mine + request
            found[step].append(jnp.sum(turned[:, at : at + 1] * block, axis=0, keepdims=True))
    power = rate
    for step in range(STEPS):
        here = slice(step * mine, (step + 1) * mine)
        total = power * jnp.concatenate(found[step], axis=0)
        power = power * rate
        factor = None
        for earlier in range(step, -1, -1):
            there = slice(earlier * mine, (earlier + 1) * mine)
            score = jnp.sum(queries[here] * keys[there], axis=-1, keepdims=True)
            if factor is not None:
                score = score * factor
            total = total + score * values[there]
            factor = rate if factor is None else factor * rate
        total = total * lax.rsqrt(jnp.mean(total * total, axis=-1, keepdims=True) + EPS)
        spiked = total * gain_ref[...] * mask_ref[step].astype(jnp.float32)
        out_ref[here, :] = spiked.astype(jnp.bfloat16)


def attention(decay, ours, theirs, state, head_gain, att_mask):
    rows, width = ours.shape
    mine, heads = state.shape[:2]
    last = width // LANES - 1
    return pl.pallas_call(
        attention_kernel,
        grid=(heads,),
        in_specs=[
            pl.BlockSpec(memory_space=pltpu.SMEM),
            pl.BlockSpec((rows, 3 * DH), lambda h: (0, h)),
            pl.BlockSpec((rows, LANES), lambda h: (0, last)),
            pl.BlockSpec((rows, 3 * DH), lambda h: (0, h)),
            pl.BlockSpec((rows, LANES), lambda h: (0, last)),
            pl.BlockSpec((mine, 1, DH, DH), lambda h: (0, h, 0, 0)),
            pl.BlockSpec((1, DH), lambda h: (0, h)),
            pl.BlockSpec((STEPS, mine, DH), lambda h: (0, 0, h)),
        ],
        out_specs=pl.BlockSpec((rows, DH), lambda h: (0, h)),
        out_shape=jax.ShapeDtypeStruct((rows, heads * DH), jnp.bfloat16),
        compiler_params=VMEM,
    )(decay, ours, ours, theirs, theirs, pltpu.with_memory_space_constraint(state, pltpu.HBM), head_gain[None, :], att_mask)


def mix_kernel(place_ref, partial_ref, inputs_ref, gain_ref, mixed_ref, hidden_ref):
    share = inputs_ref.shape[1]
    for step in range(STEPS):
        here = slice(step * share, (step + 1) * share)
        total = inputs_ref[step].astype(jnp.float32)
        for source in range(partial_ref.shape[0]):
            total = total + partial_ref[source, here, :].astype(jnp.float32)
        mixed_ref[here, :] = total
        hidden = (total * gain_ref[...]).astype(jnp.bfloat16)
        for target in range(hidden_ref.shape[0]):
            hidden_ref[target, here, :] = hidden


def mix(place, partial, inputs, gain):
    blocks, each, features = partial.shape
    whole = pl.BlockSpec((blocks, each, features), lambda i, place: (0, 0, 0))
    return pl.pallas_call(
        mix_kernel,
        grid_spec=pltpu.PrefetchScalarGridSpec(
            num_scalar_prefetch=1,
            grid=(1,),
            in_specs=[
                whole,
                pl.BlockSpec((STEPS, each // STEPS, features), lambda i, place: (0, place[3], 0)),
                pl.BlockSpec((1, features), lambda i, place: (0, 0)),
            ],
            out_specs=[pl.BlockSpec((each, features), lambda i, place: (0, 0)), whole],
        ),
        out_shape=[
            jax.ShapeDtypeStruct((each, features), jnp.float32),
            jax.ShapeDtypeStruct(partial.shape, jnp.bfloat16),
        ],
        compiler_params=VMEM,
    )(place, partial, pltpu.with_memory_space_constraint(inputs, pltpu.HBM), gain[None, :])


def gathered_product(value, weight):
    zs = lax.axis_size("z")
    half = zs // 2
    z, core = lax.axis_index("z"), lax.axis_index("core")
    towards = jnp.where(core == 0, -1, 1)
    rows, width = value.shape[0], weight.shape[1]
    out = jnp.zeros((zs, 2, rows, width), jnp.bfloat16)

    def multiply(blocks):
        return jnp.dot(blocks.reshape(-1, blocks.shape[-1]), weight, preferred_element_type=jnp.float32).astype(
            jnp.bfloat16
        ).reshape(blocks.shape[:-1] + (width,))

    def put(out, blocks, chip):
        return lax.dynamic_update_slice(out, blocks[None], ((chip + zs) % zs, 0, 0, 0))

    sibling = swap_cores(value)
    low, high = jnp.where(core == 0, value, sibling), jnp.where(core == 0, sibling, value)
    moving = jnp.stack([low, high])
    edges = edges_of(value.shape[1], GATHER_CHAINS)
    moving = [moving[..., low:high] for low, high in edges]
    weights = [weight[low:high] for low, high in edges]

    def multiply(blocks):
        total = 0.0
        for block, part in zip(blocks, weights, strict=True):
            total = total + jnp.dot(block.reshape(-1, block.shape[-1]), part, preferred_element_type=jnp.float32)
        return total.astype(jnp.bfloat16).reshape(blocks[0].shape[:-1] + (width,))

    out = put(out, multiply(moving), z)
    for distance in range(1, half):
        moving = [pass_on(part) for part in moving]
        other = [swap_cores(part) for part in moving]
        done = multiply([jnp.stack([a, b]) for a, b in zip(moving, other, strict=True)])
        out = put(out, done[0], z + towards * distance)
        out = put(out, done[1], z - towards * distance)
    return put(out, multiply([pass_on(part) for part in moving]), z + half)


def on_device(
    inputs,
    in_gain,
    qkv_weight,
    decay,
    state,
    head_gain,
    out_weight,
    mid_gain,
    up_weight,
    down_weight,
    att_mask,
    ffn_mask,
):
    blocks = lax.axis_size("core") * lax.axis_size("z")
    share = inputs.shape[1] // blocks
    features = inputs.shape[2]
    each = STEPS * share
    zs = lax.axis_size("z")
    z, core = lax.axis_index("z"), lax.axis_index("core")
    ahead = core == 0
    theirs_from = jnp.where(ahead, z + zs // 2, z + 1) % zs
    mine_from = jnp.where(ahead, z, z + zs // 2) % zs
    place = jnp.stack([theirs_from, mine_from, z * 2 + core, lax.axis_index(TENSOR)]).astype(jnp.int32)
    ours, theirs = sum_to_owner(inputs, in_gain, qkv_weight, place, ahead, True)
    spiked = attention(decay, ours, theirs, state, head_gain, att_mask)

    everyone = lax.all_gather(spiked, BATCH, axis=0, tiled=True)
    partial = jnp.dot(everyone, out_weight, preferred_element_type=jnp.float32).astype(jnp.bfloat16)
    partial = partial.reshape(blocks, each, features)
    partial = lax.all_to_all(partial, TENSOR, 0, 0, tiled=True)
    mixed, hidden = mix(place, partial, inputs, mid_gain)
    hidden = lax.all_to_all(hidden, TENSOR, 0, 0, tiled=True)
    ours, theirs = sum_to_owner(hidden, mid_gain, up_weight, place, ahead, False)
    total = ours + theirs.astype(jnp.float32)
    units = up_weight.shape[1]
    inverse = lax.rsqrt(jnp.sum(total[:, units:], axis=-1, keepdims=True) / D + EPS)
    gate = total[:, :units] * inverse
    fired = ffn_mask.reshape(each, units) * (gate / (1.0 + jnp.exp(-gate)))

    partial = gathered_product(fired.astype(jnp.bfloat16), down_weight)
    partial = lax.all_to_all(partial.reshape(blocks, each, features), TENSOR, 0, 0, tiled=True)
    final = mixed + jnp.sum(partial.astype(jnp.float32), axis=0)
    return final.astype(jnp.bfloat16).reshape(STEPS, share, features)


def solution(mesh):
    devices = mesh.devices.reshape(8, 2, 4, 4)
    inner = Mesh(devices, ("z", "core", "y", "x"))
    return jax.shard_map(
        on_device,
        mesh=inner,
        in_specs=(
            P(None, None, BATCH),
            P(BATCH),
            P(BATCH, TENSOR),
            P(TENSOR),
            P(BATCH, TENSOR, None, None),
            P(TENSOR),
            P(TENSOR, BATCH),
            P(BATCH),
            P(BATCH, TENSOR),
            P(TENSOR, BATCH),
            P(None, BATCH, TENSOR),
            P(None, BATCH, TENSOR),
        ),
        out_specs=P(None, TENSOR, BATCH),
        check_vma=False,
    )
```

profile of v0, /device:TPU:96, one launch (start us, length us, event | category | flops | bytes accessed | tf_op | source)
XLA Modules:
  0.0 188.4 jit_solution(6866849201816659413)
XLA Ops:
  0.8 2.4 %shard_map.119 = bf16[384,1664]{1,0:T(8,128)(2,1)S(1)} custom-call(s32[4]{0:T(128)S(1)} %pad_add_fusion.place_ref, bf16[3,256,512]{2,1,0:T(8,128)(2,1)} %inputs_ref.1, f32[1,512]{1,0:T(1,128)S(1)} %bitcast.131, bf16[512,1536]{1,0:T(8,128)(2,1)} %weight_ref.5), custom_call_target="tpu_custom_call" | custom-call | tf_op jit(solution)/shard_map/pallas_call | solution.py:86
  3.4 2.6 %shard_map.118 = bf16[480,1664]{1,0:T(8,128)(2,1)S(1)} custom-call(s32[4]{0:T(128)S(1)} %pad_add_fusion.place_ref, bf16[3,256,512]{2,1,0:T(8,128)(2,1)} %inputs_ref.1, f32[1,512]{1,0:T(1,128)S(1)} %bitcast.132, bf16[512,1536]{1,0:T(8,128)(2,1)} %weight_ref.5), custom_call_target="tpu_custom_call" | custom-call | tf_op jit(solution)/shard_map/pallas_call | solution.py:86
  6.5 3.2 %collective-permute-start.1 = (bf16[48,768]{1,0:T(8,128)(2,1)S(1)}, bf16[48,768]{1,0:T(8,128)(2,1)S(1)}, u32[]{:S(2)}, u32[]{:S(2)}) collective-permute-start(bf16[48,768]{1,0:T(8,128)(2,1)S(1)} %slice.323), channel_id=1, source_target_pairs={{0,32},{16,240},{32,64},{48,16},{64,96},{80,48},{96,128},{112,80},... | collective-permute-start | bytes 221192 | tf_op jit(solution)/shard_map/ppermute | solution.py:39
  11.8 3.7 %collective-permute-start.2 = (bf16[2,48,768]{2,1,0:T(8,128)(2,1)S(1)}, bf16[2,48,768]{2,1,0:T(8,128)(2,1)S(1)}, u32[]{:S(2)}, u32[]{:S(2)}) collective-permute-start(bf16[2,48,768]{2,1,0:T(8,128)(2,1)S(1)} %fusion.32), channel_id=1, source_target_pairs={{0,32},{16,240},{32,64},{48,16},{64,96},{80,48},{96,128},{112,80},... | collective-permute-start | bytes 442376 | tf_op jit(solution)/shard_map/ppermute | solution.py:39
  18.2 3.8 %collective-permute-start.3 = (bf16[2,48,768]{2,1,0:T(8,128)(2,1)S(1)}, bf16[2,48,768]{2,1,0:T(8,128)(2,1)S(1)}, u32[]{:S(2)}, u32[]{:S(2)}) collective-permute-start(bf16[2,48,768]{2,1,0:T(8,128)(2,1)S(1)} %fusion.33), channel_id=1, source_target_pairs={{0,32},{16,240},{32,64},{48,16},{64,96},{80,48},{96,128},{112,80},... | collective-permute-start | bytes 442376 | tf_op jit(solution)/shard_map/ppermute | solution.py:39
  24.7 3.8 %collective-permute-start.4 = (bf16[2,48,768]{2,1,0:T(8,128)(2,1)S(1)}, bf16[2,48,768]{2,1,0:T(8,128)(2,1)S(1)}, u32[]{:S(2)}, u32[]{:S(2)}) collective-permute-start(bf16[2,48,768]{2,1,0:T(8,128)(2,1)S(1)} %fusion.34), channel_id=1, source_target_pairs={{0,32},{16,240},{32,64},{48,16},{64,96},{80,48},{96,128},{112,80},... | collective-permute-start | bytes 442376 | tf_op jit(solution)/shard_map/ppermute | solution.py:39
  28.5 2.1 %collective-permute-start.8 = (bf16[2,48,896]{2,1,0:T(8,128)(2,1)S(1)}, bf16[2,48,896]{2,1,0:T(8,128)(2,1)S(1)}, u32[]{:S(2)}, u32[]{:S(2)}) collective-permute-start(bf16[2,48,896]{2,1,0:T(8,128)(2,1)S(1)} %fusion.29), channel_id=1, source_target_pairs={{0,32},{16,240},{32,64},{48,16},{64,96},{80,48},{96,128},{112,80},... | collective-permute-start | bytes 516104 | tf_op jit(solution)/shard_map/ppermute | solution.py:39
  31.3 2.7 %collective-permute-done.8 = bf16[2,48,896]{2,1,0:T(8,128)(2,1)S(1)} collective-permute-done((bf16[2,48,896]{2,1,0:T(8,128)(2,1)S(1)}, bf16[2,48,896]{2,1,0:T(8,128)(2,1)S(1)}, u32[]{:S(2)}, u32[]{:S(2)}) %collective-permute-start.8) | collective-permute-done | bytes 172064 | tf_op jit(solution)/shard_map/ppermute | solution.py:39
  35.5 7.2 %shard_map.120 = bf16[48,512]{1,0:T(8,128)(2,1)S(1)} custom-call(f32[4]{0:T(128)S(1)} %copy-done.6, f32[48,1664]{1,0:T(8,128)S(1)} %pad_maximum_fusion.6.ours_ref.our_sums_ref, f32[48,1664]{1,0:T(8,128)S(1)} %pad_maximum_fusion.6.ours_ref.our_sums_ref, bf16[48,1664]{1,0:T(8,128)(2,1)S(1)} %pad_maximum_fusion.8.theirs_ref.their_sums_ref, ...), custom_call_target="tpu_custom_call" | custom-call | tf_op jit(solution)/shard_map/pallas_call | solution.py:168
  42.7 18.5 %all_gather.3 = bf16[768,512]{1,0:T(8,128)(2,1)S(1)} all-gather(bf16[48,512]{1,0:T(8,128)(2,1)S(1)} %shard_map.120), channel_id=1, replica_groups=mesh['z'=8,'core'=2,'y'=4,'x'=4] {'z','core'}, dimensions={0}, use_global_device_ids=true | all-gather | bytes 835584 | tf_op jit(solution)/shard_map/all_gather | solution.py:289
  61.7 21.7 %all_to_all.15.partial_ref = bf16[16,48,512]{2,1,0:T(8,128)(2,1)S(1)} all-to-all(bf16[16,48,512]{2,1,0:T(8,128)(2,1)S(1)} %bitcast.148), channel_id=1, replica_groups=mesh['z'=8,'core'=2,'y'=4,'x'=4] {'y','x'}, dimensions={0} | all-to-all | bytes 1572864 | tf_op jit(solution)/shard_map/all_to_all | solution.py:292
  84.9 17.0 %all_to_all.16.rows_ref = bf16[16,48,512]{2,1,0:T(8,128)(2,1)S(1)} all-to-all(bf16[16,48,512]{2,1,0:T(8,128)(2,1)S(1)} %get-tuple-element.8), channel_id=1, replica_groups=mesh['z'=8,'core'=2,'y'=4,'x'=4] {'y','x'}, dimensions={0} | all-to-all | bytes 1572864 | tf_op jit(solution)/shard_map/all_to_all | solution.py:294
  111.6 2.8 %collective-permute-start.13 = (bf16[2,48,896]{2,1,0:T(8,128)(2,1)S(1)}, bf16[2,48,896]{2,1,0:T(8,128)(2,1)S(1)}, u32[]{:S(2)}, u32[]{:S(2)}) collective-permute-start(bf16[2,48,896]{2,1,0:T(8,128)(2,1)S(1)} %fusion.24), channel_id=1, source_target_pairs={{0,32},{16,240},{32,64},{48,16},{64,96},{80,48},{96,128},{112,80},... | collective-permute-start | bytes 516104 | tf_op jit(solution)/shard_map/ppermute | solution.py:39
  117.4 3.8 %collective-permute-start.14 = (bf16[2,48,896]{2,1,0:T(8,128)(2,1)S(1)}, bf16[2,48,896]{2,1,0:T(8,128)(2,1)S(1)}, u32[]{:S(2)}, u32[]{:S(2)}) collective-permute-start(bf16[2,48,896]{2,1,0:T(8,128)(2,1)S(1)} %fusion.25), channel_id=1, source_target_pairs={{0,32},{16,240},{32,64},{48,16},{64,96},{80,48},{96,128},{112,80},... | collective-permute-start | bytes 516104 | tf_op jit(solution)/shard_map/ppermute | solution.py:39
  124.2 3.8 %collective-permute-start.15 = (bf16[2,48,896]{2,1,0:T(8,128)(2,1)S(1)}, bf16[2,48,896]{2,1,0:T(8,128)(2,1)S(1)}, u32[]{:S(2)}, u32[]{:S(2)}) collective-permute-start(bf16[2,48,896]{2,1,0:T(8,128)(2,1)S(1)} %fusion.26), channel_id=1, source_target_pairs={{0,32},{16,240},{32,64},{48,16},{64,96},{80,48},{96,128},{112,80},... | collective-permute-start | bytes 516104 | tf_op jit(solution)/shard_map/ppermute | solution.py:39
  128.0 2.3 %collective-permute-start.19 = (bf16[2,48,1024]{2,1,0:T(8,128)(2,1)S(1)}, bf16[2,48,1024]{2,1,0:T(8,128)(2,1)S(1)}, u32[]{:S(2)}, u32[]{:S(2)}) collective-permute-start(bf16[2,48,1024]{2,1,0:T(8,128)(2,1)S(1)} %fusion.22), channel_id=1, source_target_pairs={{0,32},{16,240},{32,64},{48,16},{64,96},{80,48},{96,128},{112,80},... | collective-permute-start | bytes 589832 | tf_op jit(solution)/shard_map/ppermute | solution.py:39
  131.1 2.7 %collective-permute-done.19 = bf16[2,48,1024]{2,1,0:T(8,128)(2,1)S(1)} collective-permute-done((bf16[2,48,1024]{2,1,0:T(8,128)(2,1)S(1)}, bf16[2,48,1024]{2,1,0:T(8,128)(2,1)S(1)}, u32[]{:S(2)}, u32[]{:S(2)}) %collective-permute-start.19) | collective-permute-done | bytes 196640 | tf_op jit(solution)/shard_map/ppermute | solution.py:39
  137.4 3.5 %collective-permute-start.25 = (bf16[2,48,896]{2,1,0:T(8,128)(2,1)S(1)}, bf16[2,48,896]{2,1,0:T(8,128)(2,1)S(1)}, u32[]{:S(2)}, u32[]{:S(2)}) collective-permute-start(bf16[2,48,896]{2,1,0:T(8,128)(2,1)S(1)} %get-tuple-element.25), channel_id=1, source_target_pairs={{0,32},{16,240},{32,64},{48,16},{64,96},{80,48},{96,128},{112,80},... | collective-permute-start | bytes 516104 | tf_op jit(solution)/shard_map/ppermute | solution.py:39
  141.3 2.5 %collective-permute-done.25 = bf16[2,48,896]{2,1,0:T(8,128)(2,1)S(1)} collective-permute-done((bf16[2,48,896]{2,1,0:T(8,128)(2,1)S(1)}, bf16[2,48,896]{2,1,0:T(8,128)(2,1)S(1)}, u32[]{:S(2)}, u32[]{:S(2)}) %collective-permute-start.25) | collective-permute-done | bytes 172064 | tf_op jit(solution)/shard_map/ppermute | solution.py:39
  144.2 3.8 %collective-permute-start.29 = (bf16[2,48,896]{2,1,0:T(8,128)(2,1)S(1)}, bf16[2,48,896]{2,1,0:T(8,128)(2,1)S(1)}, u32[]{:S(2)}, u32[]{:S(2)}) collective-permute-start(bf16[2,48,896]{2,1,0:T(8,128)(2,1)S(1)} %collective-permute-done.25), channel_id=1, source_target_pairs={{0,32},{16,240},{32,64},{48,16},{64,96},{80,48},{96,128},{112,80},... | collective-permute-start | bytes 516104 | tf_op jit(solution)/shard_map/ppermute | solution.py:39
  151.2 2.2 %collective-permute-done.27 = bf16[2,48,896]{2,1,0:T(8,128)(2,1)S(1)} collective-permute-done((bf16[2,48,896]{2,1,0:T(8,128)(2,1)S(1)}, bf16[2,48,896]{2,1,0:T(8,128)(2,1)S(1)}, u32[]{:S(2)}, u32[]{:S(2)}) %collective-permute-start.27) | collective-permute-done | bytes 172064 | tf_op jit(solution)/shard_map/ppermute | solution.py:39
  153.4 3.0 %collective-permute-start.31 = (bf16[2,48,896]{2,1,0:T(8,128)(2,1)S(1)}, bf16[2,48,896]{2,1,0:T(8,128)(2,1)S(1)}, u32[]{:S(2)}, u32[]{:S(2)}) collective-permute-start(bf16[2,48,896]{2,1,0:T(8,128)(2,1)S(1)} %collective-permute-done.27), channel_id=1, source_target_pairs={{0,32},{16,240},{32,64},{48,16},{64,96},{80,48},{96,128},{112,80},... | collective-permute-start | bytes 516104 | tf_op jit(solution)/shard_map/ppermute | solution.py:39
  159.4 3.7 %collective-permute-start.35 = (bf16[2,48,896]{2,1,0:T(8,128)(2,1)S(1)}, bf16[2,48,896]{2,1,0:T(8,128)(2,1)S(1)}, u32[]{:S(2)}, u32[]{:S(2)}) collective-permute-start(bf16[2,48,896]{2,1,0:T(8,128)(2,1)S(1)} %collective-permute-done.31), channel_id=1, source_target_pairs={{0,32},{16,240},{32,64},{48,16},{64,96},{80,48},{96,128},{112,80},... | collective-permute-start | bytes 516104 | tf_op jit(solution)/shard_map/ppermute | solution.py:39
  169.7 18.0 %all_to_all.17 = bf16[16,48,512]{2,1,0:T(8,128)(2,1)S(1)} all-to-all(bf16[16,48,512]{2,1,0:T(8,128)(2,1)S(1)} %bitcast.134), channel_id=1, replica_groups=mesh['z'=8,'core'=2,'y'=4,'x'=4] {'y','x'}, dimensions={0} | all-to-all | bytes 1572864 | tf_op jit(solution)/shard_map/all_to_all | solution.py:303
  (161 shorter events, 47.0 us)
Async XLA Ops:
  9.7 5.8 %collective-permute-start.5 = (bf16[48,896]{1,0:T(8,128)(2,1)S(1)}, bf16[48,896]{1,0:T(8,128)(2,1)S(1)}, u32[]{:S(2)}, u32[]{:S(2)}) collective-permute-start(bf16[48,896]{1,0:T(8,128)(2,1)S(1)} %slice.330), channel_id=1, source_target_pairs={{0,32},{16,240},{32,64},{48,16},{64,96},{80,48},{96,128},{112,80},... | collective-permute-start | bytes 258056 | tf_op jit(solution)/shard_map/ppermute | solution.py:39
  11.8 6.3 %collective-permute-start.2 = (bf16[2,48,768]{2,1,0:T(8,128)(2,1)S(1)}, bf16[2,48,768]{2,1,0:T(8,128)(2,1)S(1)}, u32[]{:S(2)}, u32[]{:S(2)}) collective-permute-start(bf16[2,48,768]{2,1,0:T(8,128)(2,1)S(1)} %fusion.32), channel_id=1, source_target_pairs={{0,32},{16,240},{32,64},{48,16},{64,96},{80,48},{96,128},{112,80},... | collective-permute-start | bytes 442376 | tf_op jit(solution)/shard_map/ppermute | solution.py:39
  15.6 6.3 %collective-permute-start.6 = (bf16[2,48,896]{2,1,0:T(8,128)(2,1)S(1)}, bf16[2,48,896]{2,1,0:T(8,128)(2,1)S(1)}, u32[]{:S(2)}, u32[]{:S(2)}) collective-permute-start(bf16[2,48,896]{2,1,0:T(8,128)(2,1)S(1)} %fusion.27), channel_id=1, source_target_pairs={{0,32},{16,240},{32,64},{48,16},{64,96},{80,48},{96,128},{112,80},... | collective-permute-start | bytes 516104 | tf_op jit(solution)/shard_map/ppermute | solution.py:39
  18.2 6.4 %collective-permute-start.3 = (bf16[2,48,768]{2,1,0:T(8,128)(2,1)S(1)}, bf16[2,48,768]{2,1,0:T(8,128)(2,1)S(1)}, u32[]{:S(2)}, u32[]{:S(2)}) collective-permute-start(bf16[2,48,768]{2,1,0:T(8,128)(2,1)S(1)} %fusion.33), channel_id=1, source_target_pairs={{0,32},{16,240},{32,64},{48,16},{64,96},{80,48},{96,128},{112,80},... | collective-permute-start | bytes 442376 | tf_op jit(solution)/shard_map/ppermute | solution.py:39
  22.0 6.4 %collective-permute-start.7 = (bf16[2,48,896]{2,1,0:T(8,128)(2,1)S(1)}, bf16[2,48,896]{2,1,0:T(8,128)(2,1)S(1)}, u32[]{:S(2)}, u32[]{:S(2)}) collective-permute-start(bf16[2,48,896]{2,1,0:T(8,128)(2,1)S(1)} %fusion.28), channel_id=1, source_target_pairs={{0,32},{16,240},{32,64},{48,16},{64,96},{80,48},{96,128},{112,80},... | collective-permute-start | bytes 516104 | tf_op jit(solution)/shard_map/ppermute | solution.py:39
  24.7 6.4 %collective-permute-start.4 = (bf16[2,48,768]{2,1,0:T(8,128)(2,1)S(1)}, bf16[2,48,768]{2,1,0:T(8,128)(2,1)S(1)}, u32[]{:S(2)}, u32[]{:S(2)}) collective-permute-start(bf16[2,48,768]{2,1,0:T(8,128)(2,1)S(1)} %fusion.34), channel_id=1, source_target_pairs={{0,32},{16,240},{32,64},{48,16},{64,96},{80,48},{96,128},{112,80},... | collective-permute-start | bytes 442376 | tf_op jit(solution)/shard_map/ppermute | solution.py:39
  28.5 5.5 %collective-permute-start.8 = (bf16[2,48,896]{2,1,0:T(8,128)(2,1)S(1)}, bf16[2,48,896]{2,1,0:T(8,128)(2,1)S(1)}, u32[]{:S(2)}, u32[]{:S(2)}) collective-permute-start(bf16[2,48,896]{2,1,0:T(8,128)(2,1)S(1)} %fusion.29), channel_id=1, source_target_pairs={{0,32},{16,240},{32,64},{48,16},{64,96},{80,48},{96,128},{112,80},... | collective-permute-start | bytes 516104 | tf_op jit(solution)/shard_map/ppermute | solution.py:39
  108.6 5.9 %collective-permute-start.16 = (bf16[48,1024]{1,0:T(8,128)(2,1)S(1)}, bf16[48,1024]{1,0:T(8,128)(2,1)S(1)}, u32[]{:S(2)}, u32[]{:S(2)}) collective-permute-start(bf16[48,1024]{1,0:T(8,128)(2,1)S(1)} %slice.355), channel_id=1, source_target_pairs={{0,32},{16,240},{32,64},{48,16},{64,96},{80,48},{96,128},{112,80},... | collective-permute-start | bytes 294920 | tf_op jit(solution)/shard_map/ppermute | solution.py:39
  111.6 5.8 %collective-permute-start.13 = (bf16[2,48,896]{2,1,0:T(8,128)(2,1)S(1)}, bf16[2,48,896]{2,1,0:T(8,128)(2,1)S(1)}, u32[]{:S(2)}, u32[]{:S(2)}) collective-permute-start(bf16[2,48,896]{2,1,0:T(8,128)(2,1)S(1)} %fusion.24), channel_id=1, source_target_pairs={{0,32},{16,240},{32,64},{48,16},{64,96},{80,48},{96,128},{112,80},... | collective-permute-start | bytes 516104 | tf_op jit(solution)/shard_map/ppermute | solution.py:39
  114.6 6.6 %collective-permute-start.17 = (bf16[2,48,1024]{2,1,0:T(8,128)(2,1)S(1)}, bf16[2,48,1024]{2,1,0:T(8,128)(2,1)S(1)}, u32[]{:S(2)}, u32[]{:S(2)}) collective-permute-start(bf16[2,48,1024]{2,1,0:T(8,128)(2,1)S(1)} %fusion.20), channel_id=1, source_target_pairs={{0,32},{16,240},{32,64},{48,16},{64,96},{80,48},{96,128},{112,80},... | collective-permute-start | bytes 589832 | tf_op jit(solution)/shard_map/ppermute | solution.py:39
  117.4 6.7 %collective-permute-start.14 = (bf16[2,48,896]{2,1,0:T(8,128)(2,1)S(1)}, bf16[2,48,896]{2,1,0:T(8,128)(2,1)S(1)}, u32[]{:S(2)}, u32[]{:S(2)}) collective-permute-start(bf16[2,48,896]{2,1,0:T(8,128)(2,1)S(1)} %fusion.25), channel_id=1, source_target_pairs={{0,32},{16,240},{32,64},{48,16},{64,96},{80,48},{96,128},{112,80},... | collective-permute-start | bytes 516104 | tf_op jit(solution)/shard_map/ppermute | solution.py:39
  121.3 6.7 %collective-permute-start.18 = (bf16[2,48,1024]{2,1,0:T(8,128)(2,1)S(1)}, bf16[2,48,1024]{2,1,0:T(8,128)(2,1)S(1)}, u32[]{:S(2)}, u32[]{:S(2)}) collective-permute-start(bf16[2,48,1024]{2,1,0:T(8,128)(2,1)S(1)} %fusion.21), channel_id=1, source_target_pairs={{0,32},{16,240},{32,64},{48,16},{64,96},{80,48},{96,128},{112,80},... | collective-permute-start | bytes 589832 | tf_op jit(solution)/shard_map/ppermute | solution.py:39
  124.2 6.7 %collective-permute-start.15 = (bf16[2,48,896]{2,1,0:T(8,128)(2,1)S(1)}, bf16[2,48,896]{2,1,0:T(8,128)(2,1)S(1)}, u32[]{:S(2)}, u32[]{:S(2)}) collective-permute-start(bf16[2,48,896]{2,1,0:T(8,128)(2,1)S(1)} %fusion.26), channel_id=1, source_target_pairs={{0,32},{16,240},{32,64},{48,16},{64,96},{80,48},{96,128},{112,80},... | collective-permute-start | bytes 516104 | tf_op jit(solution)/shard_map/ppermute | solution.py:39
  128.0 5.7 %collective-permute-start.19 = (bf16[2,48,1024]{2,1,0:T(8,128)(2,1)S(1)}, bf16[2,48,1024]{2,1,0:T(8,128)(2,1)S(1)}, u32[]{:S(2)}, u32[]{:S(2)}) collective-permute-start(bf16[2,48,1024]{2,1,0:T(8,128)(2,1)S(1)} %fusion.22), channel_id=1, source_target_pairs={{0,32},{16,240},{32,64},{48,16},{64,96},{80,48},{96,128},{112,80},... | collective-permute-start | bytes 589832 | tf_op jit(solution)/shard_map/ppermute | solution.py:39
  137.4 6.5 %collective-permute-start.25 = (bf16[2,48,896]{2,1,0:T(8,128)(2,1)S(1)}, bf16[2,48,896]{2,1,0:T(8,128)(2,1)S(1)}, u32[]{:S(2)}, u32[]{:S(2)}) collective-permute-start(bf16[2,48,896]{2,1,0:T(8,128)(2,1)S(1)} %get-tuple-element.25), channel_id=1, source_target_pairs={{0,32},{16,240},{32,64},{48,16},{64,96},{80,48},{96,128},{112,80},... | collective-permute-start | bytes 516104 | tf_op jit(solution)/shard_map/ppermute | solution.py:39
  140.9 7.1 %collective-permute-start.23 = (bf16[2,48,896]{2,1,0:T(8,128)(2,1)S(1)}, bf16[2,48,896]{2,1,0:T(8,128)(2,1)S(1)}, u32[]{:S(2)}, u32[]{:S(2)}) collective-permute-start(bf16[2,48,896]{2,1,0:T(8,128)(2,1)S(1)} %get-tuple-element.26), channel_id=1, source_target_pairs={{0,32},{16,240},{32,64},{48,16},{64,96},{80,48},{96,128},{112,80},... | collective-permute-start | bytes 516104 | tf_op jit(solution)/shard_map/ppermute | solution.py:39
  143.8 5.5 %collective-permute-start.26 = (bf16[2,48,896]{2,1,0:T(8,128)(2,1)S(1)}, bf16[2,48,896]{2,1,0:T(8,128)(2,1)S(1)}, u32[]{:S(2)}, u32[]{:S(2)}) collective-permute-start(bf16[2,48,896]{2,1,0:T(8,128)(2,1)S(1)} %collective-permute-done.25), channel_id=1, source_target_pairs={{0,16},{16,0},{1,17},{17,1},{2,18},{18,2},{3,19},{19,3},{4,20},{20... | collective-permute-start | bytes 516104 | tf_op jit(solution)/shard_map/ppermute | solution.py:30
  144.2 12.3 %collective-permute-start.29 = (bf16[2,48,896]{2,1,0:T(8,128)(2,1)S(1)}, bf16[2,48,896]{2,1,0:T(8,128)(2,1)S(1)}, u32[]{:S(2)}, u32[]{:S(2)}) collective-permute-start(bf16[2,48,896]{2,1,0:T(8,128)(2,1)S(1)} %collective-permute-done.25), channel_id=1, source_target_pairs={{0,32},{16,240},{32,64},{48,16},{64,96},{80,48},{96,128},{112,80},... | collective-permute-start | bytes 516104 | tf_op jit(solution)/shard_map/ppermute | solution.py:39
  148.0 5.4 %collective-permute-start.27 = (bf16[2,48,896]{2,1,0:T(8,128)(2,1)S(1)}, bf16[2,48,896]{2,1,0:T(8,128)(2,1)S(1)}, u32[]{:S(2)}, u32[]{:S(2)}) collective-permute-start(bf16[2,48,896]{2,1,0:T(8,128)(2,1)S(1)} %collective-permute-done.23), channel_id=1, source_target_pairs={{0,32},{16,240},{32,64},{48,16},{64,96},{80,48},{96,128},{112,80},... | collective-permute-start | bytes 516104 | tf_op jit(solution)/shard_map/ppermute | solution.py:39
  153.4 6.0 %collective-permute-start.31 = (bf16[2,48,896]{2,1,0:T(8,128)(2,1)S(1)}, bf16[2,48,896]{2,1,0:T(8,128)(2,1)S(1)}, u32[]{:S(2)}, u32[]{:S(2)}) collective-permute-start(bf16[2,48,896]{2,1,0:T(8,128)(2,1)S(1)} %collective-permute-done.27), channel_id=1, source_target_pairs={{0,32},{16,240},{32,64},{48,16},{64,96},{80,48},{96,128},{112,80},... | collective-permute-start | bytes 516104 | tf_op jit(solution)/shard_map/ppermute | solution.py:39
  156.5 6.6 %collective-permute-start.33 = (bf16[2,48,896]{2,1,0:T(8,128)(2,1)S(1)}, bf16[2,48,896]{2,1,0:T(8,128)(2,1)S(1)}, u32[]{:S(2)}, u32[]{:S(2)}) collective-permute-start(bf16[2,48,896]{2,1,0:T(8,128)(2,1)S(1)} %collective-permute-done.29), channel_id=1, source_target_pairs={{0,32},{16,240},{32,64},{48,16},{64,96},{80,48},{96,128},{112,80},... | collective-permute-start | bytes 516104 | tf_op jit(solution)/shard_map/ppermute | solution.py:39
  159.4 10.0 %collective-permute-start.35 = (bf16[2,48,896]{2,1,0:T(8,128)(2,1)S(1)}, bf16[2,48,896]{2,1,0:T(8,128)(2,1)S(1)}, u32[]{:S(2)}, u32[]{:S(2)}) collective-permute-start(bf16[2,48,896]{2,1,0:T(8,128)(2,1)S(1)} %collective-permute-done.31), channel_id=1, source_target_pairs={{0,32},{16,240},{32,64},{48,16},{64,96},{80,48},{96,128},{112,80},... | collective-permute-start | bytes 516104 | tf_op jit(solution)/shard_map/ppermute | solution.py:39
  163.1 5.8 %collective-permute-start.32 = (bf16[2,48,896]{2,1,0:T(8,128)(2,1)S(1)}, bf16[2,48,896]{2,1,0:T(8,128)(2,1)S(1)}, u32[]{:S(2)}, u32[]{:S(2)}) collective-permute-start(bf16[2,48,896]{2,1,0:T(8,128)(2,1)S(1)} %collective-permute-done.31), channel_id=1, source_target_pairs={{0,16},{16,0},{1,17},{17,1},{2,18},{18,2},{3,19},{19,3},{4,20},{20... | collective-permute-start | bytes 516104 | tf_op jit(solution)/shard_map/ppermute | solution.py:30
  163.1 5.5 %collective-permute-start.36 = (bf16[2,48,896]{2,1,0:T(8,128)(2,1)S(1)}, bf16[2,48,896]{2,1,0:T(8,128)(2,1)S(1)}, u32[]{:S(2)}, u32[]{:S(2)}) collective-permute-start(bf16[2,48,896]{2,1,0:T(8,128)(2,1)S(1)} %collective-permute-done.33), channel_id=1, source_target_pairs={{0,32},{16,240},{32,64},{48,16},{64,96},{80,48},{96,128},{112,80},... | collective-permute-start | bytes 516104 | tf_op jit(solution)/shard_map/ppermute | solution.py:39
  (22 other events, 167.1 us)
where the time goes:
time: 189 us; the launch traced here: 188 us
  blocking collectives  75.1 us (40%)
  starting transfers between devices  59.1 us (31%)
  waiting for transfers between devices  27.9 us (15%)
  Pallas kernels  16.9 us (9%)
  matrix products  3.91 us (2%)
  other arithmetic  3.82 us (2%)
    ppermute x24, starting transfers between devices, pass_on(): return lax.ppermute(value, BATCH, pairs)  57.5 us
    all_to_all x1, blocking collectives, on_device(): partial = lax.all_to_all(partial, TENSOR, 0, 0, tiled=True)  21.7 us
    ppermute x24, waiting for transfers between devices, pass_on(): return lax.ppermute(value, BATCH, pairs)  19.3 us
    all_gather x1, blocking collectives, on_device(): everyone = lax.all_gather(spiked, BATCH, axis=0, tiled=True)  18.5 us
    all_to_all x1, blocking collectives, on_device(): lax.all_to_all(partial.reshape(blocks, each, features), TENSOR, 0, 0, til...  18 us
    all_to_all x1, blocking collectives, on_device(): hidden = lax.all_to_all(hidden, TENSOR, 0, 0, tiled=True)  17 us
    ppermute x13, waiting for transfers between devices, swap_cores(): return lax.ppermute(value, 'core', [(0, 1), (1, 0)])  8.59 us
    pallas_call x4, Pallas kernels, product(): pl.pallas_call(functools.partial(product_kernel, chips, first, which), in...  8.22 us
  transfers between devices with their start and end apart: 37, of which 22 were waited for; matrix products, arithmetic and copies ran while one was open for 3% of the time, Pallas kernels for 2%

commit v1 on v0

--- a/solution.py
+++ b/solution.py
@@ -136,17 +136,22 @@
     keys = parts[:, DH : 2 * DH] * scale
     values = parts[:, 2 * DH :]
     rate = decay_ref[head]
-    turned = queries.T
-    found = [[] for _ in range(STEPS)]
-    for request in range(mine):
-        block = state_ref[request, 0]
-        for step in range(STEPS):
-            at = step * mine + request
-            found[step].append(jnp.sum(turned[:, at : at + 1] * block, axis=0, keepdims=True))
+    tiled = jnp.concatenate([queries] * mine, axis=1)
+    row = lax.broadcasted_iota(jnp.int32, tiled.shape, 0) % mine
+    column = lax.broadcasted_iota(jnp.int32, tiled.shape, 1) // DH
+    left = jnp.where(row == column, tiled, 0.0)
+    left_high = left.astype(jnp.bfloat16)
+    left_low = (left - left_high.astype(jnp.float32)).astype(jnp.bfloat16)
+    right = state_ref[...].reshape(mine * DH, DH)
+    right_high = right.astype(jnp.bfloat16)
+    right_low = (right - right_high.astype(jnp.float32)).astype(jnp.bfloat16)
+    both = jnp.concatenate([left_high, left_low], axis=0)
+    found = jnp.dot(both, right_high, preferred_element_type=jnp.float32)
+    found = found[:rows] + found[rows:] + jnp.dot(left_high, right_low, preferred_element_type=jnp.float32)
     power = rate
     for step in range(STEPS):
         here = slice(step * mine, (step + 1) * mine)
-        total = power * jnp.concatenate(found[step], axis=0)
+        total = power * found[here]
         power = power * rate
         factor = None
         for earlier in range(step, -1, -1):

time: 189 us -> 186 us (0.984)
  Pallas kernels: 16.9 us -> 14.3 us
    pallas_call x1, Pallas kernels: 7.18 us -> 4.53 us  [attention(): pl.pallas_call(attention_kernel, grid=(heads,), in_specs=[pl.BlockSpec(me...]
where the time goes in v1:
time: 186 us
  blocking collectives  74.9 us (40%)
  starting transfers between devices  59.1 us (32%)
  waiting for transfers between devices  27.9 us (15%)
  Pallas kernels  14.3 us (8%)
  matrix products  3.91 us (2%)
  other arithmetic  3.82 us (2%)
    ppermute x24, starting transfers between devices, pass_on(): return lax.ppermute(value, BATCH, pairs)  57.7 us
    all_to_all x1, blocking collectives, on_device(): partial = lax.all_to_all(partial, TENSOR, 0, 0, tiled=True)  21.7 us
    ppermute x24, waiting for transfers between devices, pass_on(): return lax.ppermute(value, BATCH, pairs)  19.3 us
    all_gather x1, blocking collectives, on_device(): everyone = lax.all_gather(spiked, BATCH, axis=0, tiled=True)  18.3 us
    all_to_all x1, blocking collectives, on_device(): lax.all_to_all(partial.reshape(blocks, each, features), TENSOR, 0, 0, til...  18 us
    all_to_all x1, blocking collectives, on_device(): hidden = lax.all_to_all(hidden, TENSOR, 0, 0, tiled=True)  17 us
    ppermute x13, waiting for transfers between devices, swap_cores(): return lax.ppermute(value, 'core', [(0, 1), (1, 0)])  8.59 us
    pallas_call x4, Pallas kernels, product(): pl.pallas_call(functools.partial(product_kernel, chips, first, which), in...  8.22 us
  transfers between devices with their start and end apart: 37, of which 22 were waited for; matrix products, arithmetic and copies ran while one was open for 3% of the time, Pallas kernels for 2%

profile of v1, /device:TPU:96, one launch (start us, length us, event | category | flops | bytes accessed | tf_op | source)
XLA Modules:
  0.0 185.6 jit_solution(4494677249410049519)
XLA Ops:
  0.8 2.4 %shard_map.119 = bf16[384,1664]{1,0:T(8,128)(2,1)S(1)} custom-call(s32[4]{0:T(128)S(1)} %pad_add_fusion.place_ref, bf16[3,256,512]{2,1,0:T(8,128)(2,1)} %inputs_ref.1, f32[1,512]{1,0:T(1,128)S(1)} %bitcast.131, bf16[512,1536]{1,0:T(8,128)(2,1)} %weight_ref.5), custom_call_target="tpu_custom_call" | custom-call | tf_op jit(solution)/shard_map/pallas_call | solution.py:86
  3.4 2.6 %shard_map.118 = bf16[480,1664]{1,0:T(8,128)(2,1)S(1)} custom-call(s32[4]{0:T(128)S(1)} %pad_add_fusion.place_ref, bf16[3,256,512]{2,1,0:T(8,128)(2,1)} %inputs_ref.1, f32[1,512]{1,0:T(1,128)S(1)} %bitcast.132, bf16[512,1536]{1,0:T(8,128)(2,1)} %weight_ref.5), custom_call_target="tpu_custom_call" | custom-call | tf_op jit(solution)/shard_map/pallas_call | solution.py:86
  6.5 3.2 %collective-permute-start.1 = (bf16[48,768]{1,0:T(8,128)(2,1)S(1)}, bf16[48,768]{1,0:T(8,128)(2,1)S(1)}, u32[]{:S(2)}, u32[]{:S(2)}) collective-permute-start(bf16[48,768]{1,0:T(8,128)(2,1)S(1)} %slice.323), channel_id=1, source_target_pairs={{0,32},{16,240},{32,64},{48,16},{64,96},{80,48},{96,128},{112,80},... | collective-permute-start | bytes 221192 | tf_op jit(solution)/shard_map/ppermute | solution.py:39
  11.8 3.7 %collective-permute-start.2 = (bf16[2,48,768]{2,1,0:T(8,128)(2,1)S(1)}, bf16[2,48,768]{2,1,0:T(8,128)(2,1)S(1)}, u32[]{:S(2)}, u32[]{:S(2)}) collective-permute-start(bf16[2,48,768]{2,1,0:T(8,128)(2,1)S(1)} %fusion.32), channel_id=1, source_target_pairs={{0,32},{16,240},{32,64},{48,16},{64,96},{80,48},{96,128},{112,80},... | collective-permute-start | bytes 442376 | tf_op jit(solution)/shard_map/ppermute | solution.py:39
  18.2 3.8 %collective-permute-start.3 = (bf16[2,48,768]{2,1,0:T(8,128)(2,1)S(1)}, bf16[2,48,768]{2,1,0:T(8,128)(2,1)S(1)}, u32[]{:S(2)}, u32[]{:S(2)}) collective-permute-start(bf16[2,48,768]{2,1,0:T(8,128)(2,1)S(1)} %fusion.33), channel_id=1, source_target_pairs={{0,32},{16,240},{32,64},{48,16},{64,96},{80,48},{96,128},{112,80},... | collective-permute-start | bytes 442376 | tf_op jit(solution)/shard_map/ppermute | solution.py:39
  24.7 3.8 %collective-permute-start.4 = (bf16[2,48,768]{2,1,0:T(8,128)(2,1)S(1)}, bf16[2,48,768]{2,1,0:T(8,128)(2,1)S(1)}, u32[]{:S(2)}, u32[]{:S(2)}) collective-permute-start(bf16[2,48,768]{2,1,0:T(8,128)(2,1)S(1)} %fusion.34), channel_id=1, source_target_pairs={{0,32},{16,240},{32,64},{48,16},{64,96},{80,48},{96,128},{112,80},... | collective-permute-start | bytes 442376 | tf_op jit(solution)/shard_map/ppermute | solution.py:39
  28.5 2.1 %collective-permute-start.8 = (bf16[2,48,896]{2,1,0:T(8,128)(2,1)S(1)}, bf16[2,48,896]{2,1,0:T(8,128)(2,1)S(1)}, u32[]{:S(2)}, u32[]{:S(2)}) collective-permute-start(bf16[2,48,896]{2,1,0:T(8,128)(2,1)S(1)} %fusion.29), channel_id=1, source_target_pairs={{0,32},{16,240},{32,64},{48,16},{64,96},{80,48},{96,128},{112,80},... | collective-permute-start | bytes 516104 | tf_op jit(solution)/shard_map/ppermute | solution.py:39
  31.3 2.7 %collective-permute-done.8 = bf16[2,48,896]{2,1,0:T(8,128)(2,1)S(1)} collective-permute-done((bf16[2,48,896]{2,1,0:T(8,128)(2,1)S(1)}, bf16[2,48,896]{2,1,0:T(8,128)(2,1)S(1)}, u32[]{:S(2)}, u32[]{:S(2)}) %collective-permute-start.8) | collective-permute-done | bytes 172064 | tf_op jit(solution)/shard_map/ppermute | solution.py:39
  35.5 4.5 %shard_map.120 = bf16[48,512]{1,0:T(8,128)(2,1)S(1)} custom-call(f32[4]{0:T(128)S(1)} %copy-done.6, f32[48,1664]{1,0:T(8,128)S(1)} %pad_maximum_fusion.6.ours_ref.our_sums_ref, f32[48,1664]{1,0:T(8,128)S(1)} %pad_maximum_fusion.6.ours_ref.our_sums_ref, bf16[48,1664]{1,0:T(8,128)(2,1)S(1)} %pad_maximum_fusion.8.theirs_ref.their_sums_ref, ...), custom_call_target="tpu_custom_call" | custom-call | tf_op jit(solution)/shard_map/pallas_call | solution.py:173
  40.0 18.3 %all_gather.3 = bf16[768,512]{1,0:T(8,128)(2,1)S(1)} all-gather(bf16[48,512]{1,0:T(8,128)(2,1)S(1)} %shard_map.120), channel_id=1, replica_groups=mesh['z'=8,'core'=2,'y'=4,'x'=4] {'z','core'}, dimensions={0}, use_global_device_ids=true | all-gather | bytes 835584 | tf_op jit(solution)/shard_map/all_gather | solution.py:294
  58.9 21.7 %all_to_all.15.partial_ref = bf16[16,48,512]{2,1,0:T(8,128)(2,1)S(1)} all-to-all(bf16[16,48,512]{2,1,0:T(8,128)(2,1)S(1)} %bitcast.148), channel_id=1, replica_groups=mesh['z'=8,'core'=2,'y'=4,'x'=4] {'y','x'}, dimensions={0} | all-to-all | bytes 1572864 | tf_op jit(solution)/shard_map/all_to_all | solution.py:297
  82.1 17.0 %all_to_all.16.rows_ref = bf16[16,48,512]{2,1,0:T(8,128)(2,1)S(1)} all-to-all(bf16[16,48,512]{2,1,0:T(8,128)(2,1)S(1)} %get-tuple-element.8), channel_id=1, replica_groups=mesh['z'=8,'core'=2,'y'=4,'x'=4] {'y','x'}, dimensions={0} | all-to-all | bytes 1572864 | tf_op jit(solution)/shard_map/all_to_all | solution.py:299
  108.8 2.8 %collective-permute-start.13 = (bf16[2,48,896]{2,1,0:T(8,128)(2,1)S(1)}, bf16[2,48,896]{2,1,0:T(8,128)(2,1)S(1)}, u32[]{:S(2)}, u32[]{:S(2)}) collective-permute-start(bf16[2,48,896]{2,1,0:T(8,128)(2,1)S(1)} %fusion.24), channel_id=1, source_target_pairs={{0,32},{16,240},{32,64},{48,16},{64,96},{80,48},{96,128},{112,80},... | collective-permute-start | bytes 516104 | tf_op jit(solution)/shard_map/ppermute | solution.py:39
  114.6 3.8 %collective-permute-start.14 = (bf16[2,48,896]{2,1,0:T(8,128)(2,1)S(1)}, bf16[2,48,896]{2,1,0:T(8,128)(2,1)S(1)}, u32[]{:S(2)}, u32[]{:S(2)}) collective-permute-start(bf16[2,48,896]{2,1,0:T(8,128)(2,1)S(1)} %fusion.25), channel_id=1, source_target_pairs={{0,32},{16,240},{32,64},{48,16},{64,96},{80,48},{96,128},{112,80},... | collective-permute-start | bytes 516104 | tf_op jit(solution)/shard_map/ppermute | solution.py:39
  121.3 3.8 %collective-permute-start.15 = (bf16[2,48,896]{2,1,0:T(8,128)(2,1)S(1)}, bf16[2,48,896]{2,1,0:T(8,128)(2,1)S(1)}, u32[]{:S(2)}, u32[]{:S(2)}) collective-permute-start(bf16[2,48,896]{2,1,0:T(8,128)(2,1)S(1)} %fusion.26), channel_id=1, source_target_pairs={{0,32},{16,240},{32,64},{48,16},{64,96},{80,48},{96,128},{112,80},... | collective-permute-start | bytes 516104 | tf_op jit(solution)/shard_map/ppermute | solution.py:39
  125.2 2.3 %collective-permute-start.19 = (bf16[2,48,1024]{2,1,0:T(8,128)(2,1)S(1)}, bf16[2,48,1024]{2,1,0:T(8,128)(2,1)S(1)}, u32[]{:S(2)}, u32[]{:S(2)}) collective-permute-start(bf16[2,48,1024]{2,1,0:T(8,128)(2,1)S(1)} %fusion.22), channel_id=1, source_target_pairs={{0,32},{16,240},{32,64},{48,16},{64,96},{80,48},{96,128},{112,80},... | collective-permute-start | bytes 589832 | tf_op jit(solution)/shard_map/ppermute | solution.py:39
  128.2 2.7 %collective-permute-done.19 = bf16[2,48,1024]{2,1,0:T(8,128)(2,1)S(1)} collective-permute-done((bf16[2,48,1024]{2,1,0:T(8,128)(2,1)S(1)}, bf16[2,48,1024]{2,1,0:T(8,128)(2,1)S(1)}, u32[]{:S(2)}, u32[]{:S(2)}) %collective-permute-start.19) | collective-permute-done | bytes 196640 | tf_op jit(solution)/shard_map/ppermute | solution.py:39
  134.3 3.8 %collective-permute-start.25 = (bf16[2,48,896]{2,1,0:T(8,128)(2,1)S(1)}, bf16[2,48,896]{2,1,0:T(8,128)(2,1)S(1)}, u32[]{:S(2)}, u32[]{:S(2)}) collective-permute-start(bf16[2,48,896]{2,1,0:T(8,128)(2,1)S(1)} %get-tuple-element.25), channel_id=1, source_target_pairs={{0,32},{16,240},{32,64},{48,16},{64,96},{80,48},{96,128},{112,80},... | collective-permute-start | bytes 516104 | tf_op jit(solution)/shard_map/ppermute | solution.py:39
  138.5 2.5 %collective-permute-done.25 = bf16[2,48,896]{2,1,0:T(8,128)(2,1)S(1)} collective-permute-done((bf16[2,48,896]{2,1,0:T(8,128)(2,1)S(1)}, bf16[2,48,896]{2,1,0:T(8,128)(2,1)S(1)}, u32[]{:S(2)}, u32[]{:S(2)}) %collective-permute-start.25) | collective-permute-done | bytes 172064 | tf_op jit(solution)/shard_map/ppermute | solution.py:39
  141.4 3.8 %collective-permute-start.29 = (bf16[2,48,896]{2,1,0:T(8,128)(2,1)S(1)}, bf16[2,48,896]{2,1,0:T(8,128)(2,1)S(1)}, u32[]{:S(2)}, u32[]{:S(2)}) collective-permute-start(bf16[2,48,896]{2,1,0:T(8,128)(2,1)S(1)} %collective-permute-done.25), channel_id=1, source_target_pairs={{0,32},{16,240},{32,64},{48,16},{64,96},{80,48},{96,128},{112,80},... | collective-permute-start | bytes 516104 | tf_op jit(solution)/shard_map/ppermute | solution.py:39
  148.4 2.2 %collective-permute-done.27 = bf16[2,48,896]{2,1,0:T(8,128)(2,1)S(1)} collective-permute-done((bf16[2,48,896]{2,1,0:T(8,128)(2,1)S(1)}, bf16[2,48,896]{2,1,0:T(8,128)(2,1)S(1)}, u32[]{:S(2)}, u32[]{:S(2)}) %collective-permute-start.27) | collective-permute-done | bytes 172064 | tf_op jit(solution)/shard_map/ppermute | solution.py:39
  150.6 3.0 %collective-permute-start.31 = (bf16[2,48,896]{2,1,0:T(8,128)(2,1)S(1)}, bf16[2,48,896]{2,1,0:T(8,128)(2,1)S(1)}, u32[]{:S(2)}, u32[]{:S(2)}) collective-permute-start(bf16[2,48,896]{2,1,0:T(8,128)(2,1)S(1)} %collective-permute-done.27), channel_id=1, source_target_pairs={{0,32},{16,240},{32,64},{48,16},{64,96},{80,48},{96,128},{112,80},... | collective-permute-start | bytes 516104 | tf_op jit(solution)/shard_map/ppermute | solution.py:39
  156.6 3.7 %collective-permute-start.35 = (bf16[2,48,896]{2,1,0:T(8,128)(2,1)S(1)}, bf16[2,48,896]{2,1,0:T(8,128)(2,1)S(1)}, u32[]{:S(2)}, u32[]{:S(2)}) collective-permute-start(bf16[2,48,896]{2,1,0:T(8,128)(2,1)S(1)} %collective-permute-done.31), channel_id=1, source_target_pairs={{0,32},{16,240},{32,64},{48,16},{64,96},{80,48},{96,128},{112,80},... | collective-permute-start | bytes 516104 | tf_op jit(solution)/shard_map/ppermute | solution.py:39
  166.9 18.0 %all_to_all.17 = bf16[16,48,512]{2,1,0:T(8,128)(2,1)S(1)} all-to-all(bf16[16,48,512]{2,1,0:T(8,128)(2,1)S(1)} %bitcast.134), channel_id=1, replica_groups=mesh['z'=8,'core'=2,'y'=4,'x'=4] {'y','x'}, dimensions={0} | all-to-all | bytes 1572864 | tf_op jit(solution)/shard_map/all_to_all | solution.py:308
  (161 shorter events, 46.8 us)
Async XLA Ops:
  9.7 5.8 %collective-permute-start.5 = (bf16[48,896]{1,0:T(8,128)(2,1)S(1)}, bf16[48,896]{1,0:T(8,128)(2,1)S(1)}, u32[]{:S(2)}, u32[]{:S(2)}) collective-permute-start(bf16[48,896]{1,0:T(8,128)(2,1)S(1)} %slice.330), channel_id=1, source_target_pairs={{0,32},{16,240},{32,64},{48,16},{64,96},{80,48},{96,128},{112,80},... | collective-permute-start | bytes 258056 | tf_op jit(solution)/shard_map/ppermute | solution.py:39
  11.8 6.3 %collective-permute-start.2 = (bf16[2,48,768]{2,1,0:T(8,128)(2,1)S(1)}, bf16[2,48,768]{2,1,0:T(8,128)(2,1)S(1)}, u32[]{:S(2)}, u32[]{:S(2)}) collective-permute-start(bf16[2,48,768]{2,1,0:T(8,128)(2,1)S(1)} %fusion.32), channel_id=1, source_target_pairs={{0,32},{16,240},{32,64},{48,16},{64,96},{80,48},{96,128},{112,80},... | collective-permute-start | bytes 442376 | tf_op jit(solution)/shard_map/ppermute | solution.py:39
  15.6 6.3 %collective-permute-start.6 = (bf16[2,48,896]{2,1,0:T(8,128)(2,1)S(1)}, bf16[2,48,896]{2,1,0:T(8,128)(2,1)S(1)}, u32[]{:S(2)}, u32[]{:S(2)}) collective-permute-start(bf16[2,48,896]{2,1,0:T(8,128)(2,1)S(1)} %fusion.27), channel_id=1, source_target_pairs={{0,32},{16,240},{32,64},{48,16},{64,96},{80,48},{96,128},{112,80},... | collective-permute-start | bytes 516104 | tf_op jit(solution)/shard_map/ppermute | solution.py:39
  18.2 6.4 %collective-permute-start.3 = (bf16[2,48,768]{2,1,0:T(8,128)(2,1)S(1)}, bf16[2,48,768]{2,1,0:T(8,128)(2,1)S(1)}, u32[]{:S(2)}, u32[]{:S(2)}) collective-permute-start(bf16[2,48,768]{2,1,0:T(8,128)(2,1)S(1)} %fusion.33), channel_id=1, source_target_pairs={{0,32},{16,240},{32,64},{48,16},{64,96},{80,48},{96,128},{112,80},... | collective-permute-start | bytes 442376 | tf_op jit(solution)/shard_map/ppermute | solution.py:39
  22.0 6.4 %collective-permute-start.7 = (bf16[2,48,896]{2,1,0:T(8,128)(2,1)S(1)}, bf16[2,48,896]{2,1,0:T(8,128)(2,1)S(1)}, u32[]{:S(2)}, u32[]{:S(2)}) collective-permute-start(bf16[2,48,896]{2,1,0:T(8,128)(2,1)S(1)} %fusion.28), channel_id=1, source_target_pairs={{0,32},{16,240},{32,64},{48,16},{64,96},{80,48},{96,128},{112,80},... | collective-permute-start | bytes 516104 | tf_op jit(solution)/shard_map/ppermute | solution.py:39
  24.7 6.4 %collective-permute-start.4 = (bf16[2,48,768]{2,1,0:T(8,128)(2,1)S(1)}, bf16[2,48,768]{2,1,0:T(8,128)(2,1)S(1)}, u32[]{:S(2)}, u32[]{:S(2)}) collective-permute-start(bf16[2,48,768]{2,1,0:T(8,128)(2,1)S(1)} %fusion.34), channel_id=1, source_target_pairs={{0,32},{16,240},{32,64},{48,16},{64,96},{80,48},{96,128},{112,80},... | collective-permute-start | bytes 442376 | tf_op jit(solution)/shard_map/ppermute | solution.py:39
  28.5 5.5 %collective-permute-start.8 = (bf16[2,48,896]{2,1,0:T(8,128)(2,1)S(1)}, bf16[2,48,896]{2,1,0:T(8,128)(2,1)S(1)}, u32[]{:S(2)}, u32[]{:S(2)}) collective-permute-start(bf16[2,48,896]{2,1,0:T(8,128)(2,1)S(1)} %fusion.29), channel_id=1, source_target_pairs={{0,32},{16,240},{32,64},{48,16},{64,96},{80,48},{96,128},{112,80},... | collective-permute-start | bytes 516104 | tf_op jit(solution)/shard_map/ppermute | solution.py:39
  105.7 5.9 %collective-permute-start.16 = (bf16[48,1024]{1,0:T(8,128)(2,1)S(1)}, bf16[48,1024]{1,0:T(8,128)(2,1)S(1)}, u32[]{:S(2)}, u32[]{:S(2)}) collective-permute-start(bf16[48,1024]{1,0:T(8,128)(2,1)S(1)} %slice.355), channel_id=1, source_target_pairs={{0,32},{16,240},{32,64},{48,16},{64,96},{80,48},{96,128},{112,80},... | collective-permute-start | bytes 294920 | tf_op jit(solution)/shard_map/ppermute | solution.py:39
  108.8 5.8 %collective-permute-start.13 = (bf16[2,48,896]{2,1,0:T(8,128)(2,1)S(1)}, bf16[2,48,896]{2,1,0:T(8,128)(2,1)S(1)}, u32[]{:S(2)}, u32[]{:S(2)}) collective-permute-start(bf16[2,48,896]{2,1,0:T(8,128)(2,1)S(1)} %fusion.24), channel_id=1, source_target_pairs={{0,32},{16,240},{32,64},{48,16},{64,96},{80,48},{96,128},{112,80},... | collective-permute-start | bytes 516104 | tf_op jit(solution)/shard_map/ppermute | solution.py:39
  111.8 6.6 %collective-permute-start.17 = (bf16[2,48,1024]{2,1,0:T(8,128)(2,1)S(1)}, bf16[2,48,1024]{2,1,0:T(8,128)(2,1)S(1)}, u32[]{:S(2)}, u32[]{:S(2)}) collective-permute-start(bf16[2,48,1024]{2,1,0:T(8,128)(2,1)S(1)} %fusion.20), channel_id=1, source_target_pairs={{0,32},{16,240},{32,64},{48,16},{64,96},{80,48},{96,128},{112,80},... | collective-permute-start | bytes 589832 | tf_op jit(solution)/shard_map/ppermute | solution.py:39
  114.6 6.7 %collective-permute-start.14 = (bf16[2,48,896]{2,1,0:T(8,128)(2,1)S(1)}, bf16[2,48,896]{2,1,0:T(8,128)(2,1)S(1)}, u32[]{:S(2)}, u32[]{:S(2)}) collective-permute-start(bf16[2,48,896]{2,1,0:T(8,128)(2,1)S(1)} %fusion.25), channel_id=1, source_target_pairs={{0,32},{16,240},{32,64},{48,16},{64,96},{80,48},{96,128},{112,80},... | collective-permute-start | bytes 516104 | tf_op jit(solution)/shard_map/ppermute | solution.py:39
  118.4 6.7 %collective-permute-start.18 = (bf16[2,48,1024]{2,1,0:T(8,128)(2,1)S(1)}, bf16[2,48,1024]{2,1,0:T(8,128)(2,1)S(1)}, u32[]{:S(2)}, u32[]{:S(2)}) collective-permute-start(bf16[2,48,1024]{2,1,0:T(8,128)(2,1)S(1)} %fusion.21), channel_id=1, source_target_pairs={{0,32},{16,240},{32,64},{48,16},{64,96},{80,48},{96,128},{112,80},... | collective-permute-start | bytes 589832 | tf_op jit(solution)/shard_map/ppermute | solution.py:39
  121.3 6.7 %collective-permute-start.15 = (bf16[2,48,896]{2,1,0:T(8,128)(2,1)S(1)}, bf16[2,48,896]{2,1,0:T(8,128)(2,1)S(1)}, u32[]{:S(2)}, u32[]{:S(2)}) collective-permute-start(bf16[2,48,896]{2,1,0:T(8,128)(2,1)S(1)} %fusion.26), channel_id=1, source_target_pairs={{0,32},{16,240},{32,64},{48,16},{64,96},{80,48},{96,128},{112,80},... | collective-permute-start | bytes 516104 | tf_op jit(solution)/shard_map/ppermute | solution.py:39
  125.2 5.7 %collective-permute-start.19 = (bf16[2,48,1024]{2,1,0:T(8,128)(2,1)S(1)}, bf16[2,48,1024]{2,1,0:T(8,128)(2,1)S(1)}, u32[]{:S(2)}, u32[]{:S(2)}) collective-permute-start(bf16[2,48,1024]{2,1,0:T(8,128)(2,1)S(1)} %fusion.22), channel_id=1, source_target_pairs={{0,32},{16,240},{32,64},{48,16},{64,96},{80,48},{96,128},{112,80},... | collective-permute-start | bytes 589832 | tf_op jit(solution)/shard_map/ppermute | solution.py:39
  134.3 6.7 %collective-permute-start.25 = (bf16[2,48,896]{2,1,0:T(8,128)(2,1)S(1)}, bf16[2,48,896]{2,1,0:T(8,128)(2,1)S(1)}, u32[]{:S(2)}, u32[]{:S(2)}) collective-permute-start(bf16[2,48,896]{2,1,0:T(8,128)(2,1)S(1)} %get-tuple-element.25), channel_id=1, source_target_pairs={{0,32},{16,240},{32,64},{48,16},{64,96},{80,48},{96,128},{112,80},... | collective-permute-start | bytes 516104 | tf_op jit(solution)/shard_map/ppermute | solution.py:39
  138.1 7.1 %collective-permute-start.23 = (bf16[2,48,896]{2,1,0:T(8,128)(2,1)S(1)}, bf16[2,48,896]{2,1,0:T(8,128)(2,1)S(1)}, u32[]{:S(2)}, u32[]{:S(2)}) collective-permute-start(bf16[2,48,896]{2,1,0:T(8,128)(2,1)S(1)} %get-tuple-element.26), channel_id=1, source_target_pairs={{0,32},{16,240},{32,64},{48,16},{64,96},{80,48},{96,128},{112,80},... | collective-permute-start | bytes 516104 | tf_op jit(solution)/shard_map/ppermute | solution.py:39
  141.0 5.5 %collective-permute-start.26 = (bf16[2,48,896]{2,1,0:T(8,128)(2,1)S(1)}, bf16[2,48,896]{2,1,0:T(8,128)(2,1)S(1)}, u32[]{:S(2)}, u32[]{:S(2)}) collective-permute-start(bf16[2,48,896]{2,1,0:T(8,128)(2,1)S(1)} %collective-permute-done.25), channel_id=1, source_target_pairs={{0,16},{16,0},{1,17},{17,1},{2,18},{18,2},{3,19},{19,3},{4,20},{20... | collective-permute-start | bytes 516104 | tf_op jit(solution)/shard_map/ppermute | solution.py:30
  141.4 12.3 %collective-permute-start.29 = (bf16[2,48,896]{2,1,0:T(8,128)(2,1)S(1)}, bf16[2,48,896]{2,1,0:T(8,128)(2,1)S(1)}, u32[]{:S(2)}, u32[]{:S(2)}) collective-permute-start(bf16[2,48,896]{2,1,0:T(8,128)(2,1)S(1)} %collective-permute-done.25), channel_id=1, source_target_pairs={{0,32},{16,240},{32,64},{48,16},{64,96},{80,48},{96,128},{112,80},... | collective-permute-start | bytes 516104 | tf_op jit(solution)/shard_map/ppermute | solution.py:39
  145.2 5.4 %collective-permute-start.27 = (bf16[2,48,896]{2,1,0:T(8,128)(2,1)S(1)}, bf16[2,48,896]{2,1,0:T(8,128)(2,1)S(1)}, u32[]{:S(2)}, u32[]{:S(2)}) collective-permute-start(bf16[2,48,896]{2,1,0:T(8,128)(2,1)S(1)} %collective-permute-done.23), channel_id=1, source_target_pairs={{0,32},{16,240},{32,64},{48,16},{64,96},{80,48},{96,128},{112,80},... | collective-permute-start | bytes 516104 | tf_op jit(solution)/shard_map/ppermute | solution.py:39
  150.6 6.0 %collective-permute-start.31 = (bf16[2,48,896]{2,1,0:T(8,128)(2,1)S(1)}, bf16[2,48,896]{2,1,0:T(8,128)(2,1)S(1)}, u32[]{:S(2)}, u32[]{:S(2)}) collective-permute-start(bf16[2,48,896]{2,1,0:T(8,128)(2,1)S(1)} %collective-permute-done.27), channel_id=1, source_target_pairs={{0,32},{16,240},{32,64},{48,16},{64,96},{80,48},{96,128},{112,80},... | collective-permute-start | bytes 516104 | tf_op jit(solution)/shard_map/ppermute | solution.py:39
  153.7 6.6 %collective-permute-start.33 = (bf16[2,48,896]{2,1,0:T(8,128)(2,1)S(1)}, bf16[2,48,896]{2,1,0:T(8,128)(2,1)S(1)}, u32[]{:S(2)}, u32[]{:S(2)}) collective-permute-start(bf16[2,48,896]{2,1,0:T(8,128)(2,1)S(1)} %collective-permute-done.29), channel_id=1, source_target_pairs={{0,32},{16,240},{32,64},{48,16},{64,96},{80,48},{96,128},{112,80},... | collective-permute-start | bytes 516104 | tf_op jit(solution)/shard_map/ppermute | solution.py:39
  156.6 10.0 %collective-permute-start.35 = (bf16[2,48,896]{2,1,0:T(8,128)(2,1)S(1)}, bf16[2,48,896]{2,1,0:T(8,128)(2,1)S(1)}, u32[]{:S(2)}, u32[]{:S(2)}) collective-permute-start(bf16[2,48,896]{2,1,0:T(8,128)(2,1)S(1)} %collective-permute-done.31), channel_id=1, source_target_pairs={{0,32},{16,240},{32,64},{48,16},{64,96},{80,48},{96,128},{112,80},... | collective-permute-start | bytes 516104 | tf_op jit(solution)/shard_map/ppermute | solution.py:39
  160.3 5.8 %collective-permute-start.32 = (bf16[2,48,896]{2,1,0:T(8,128)(2,1)S(1)}, bf16[2,48,896]{2,1,0:T(8,128)(2,1)S(1)}, u32[]{:S(2)}, u32[]{:S(2)}) collective-permute-start(bf16[2,48,896]{2,1,0:T(8,128)(2,1)S(1)} %collective-permute-done.31), channel_id=1, source_target_pairs={{0,16},{16,0},{1,17},{17,1},{2,18},{18,2},{3,19},{19,3},{4,20},{20... | collective-permute-start | bytes 516104 | tf_op jit(solution)/shard_map/ppermute | solution.py:30
  160.3 5.5 %collective-permute-start.36 = (bf16[2,48,896]{2,1,0:T(8,128)(2,1)S(1)}, bf16[2,48,896]{2,1,0:T(8,128)(2,1)S(1)}, u32[]{:S(2)}, u32[]{:S(2)}) collective-permute-start(bf16[2,48,896]{2,1,0:T(8,128)(2,1)S(1)} %collective-permute-done.33), channel_id=1, source_target_pairs={{0,32},{16,240},{32,64},{48,16},{64,96},{80,48},{96,128},{112,80},... | collective-permute-start | bytes 516104 | tf_op jit(solution)/shard_map/ppermute | solution.py:39
  (22 other events, 164.1 us)

commit v2 on v1

--- a/solution.py
+++ b/solution.py
@@ -147,7 +147,8 @@
     right_low = (right - right_high.astype(jnp.float32)).astype(jnp.bfloat16)
     both = jnp.concatenate([left_high, left_low], axis=0)
     found = jnp.dot(both, right_high, preferred_element_type=jnp.float32)
-    found = found[:rows] + found[rows:] + jnp.dot(left_high, right_low, preferred_element_type=jnp.float32)
+    found = found + jnp.dot(both, right_low, preferred_element_type=jnp.float32)
+    found = found[:rows] + found[rows:]
     power = rate
     for step in range(STEPS):
         here = slice(step * mine, (step + 1) * mine)

time: 186 us -> 186 us (level)
  no operation moved by 1% of the time
where the time goes in v2:
time: 186 us
  blocking collectives  74.9 us (40%)
  starting transfers between devices  59.1 us (32%)
  waiting for transfers between devices  27.9 us (15%)
  Pallas kernels  14.3 us (8%)
  matrix products  3.92 us (2%)
  other arithmetic  3.82 us (2%)
    ppermute x24, starting transfers between devices, pass_on(): return lax.ppermute(value, BATCH, pairs)  57.7 us
    all_to_all x1, blocking collectives, on_device(): partial = lax.all_to_all(partial, TENSOR, 0, 0, tiled=True)  21.7 us
    ppermute x24, waiting for transfers between devices, pass_on(): return lax.ppermute(value, BATCH, pairs)  19.3 us
    all_gather x1, blocking collectives, on_device(): everyone = lax.all_gather(spiked, BATCH, axis=0, tiled=True)  18.3 us
    all_to_all x1, blocking collectives, on_device(): lax.all_to_all(partial.reshape(blocks, each, features), TENSOR, 0, 0, til...  18 us
    all_to_all x1, blocking collectives, on_device(): hidden = lax.all_to_all(hidden, TENSOR, 0, 0, tiled=True)  17 us
    ppermute x13, waiting for transfers between devices, swap_cores(): return lax.ppermute(value, 'core', [(0, 1), (1, 0)])  8.59 us
    pallas_call x4, Pallas kernels, product(): pl.pallas_call(functools.partial(product_kernel, chips, first, which), in...  8.22 us
  transfers between devices with their start and end apart: 37, of which 22 were waited for; matrix products, arithmetic and copies ran while one was open for 3% of the time, Pallas kernels for 2%

profile of v2, /device:TPU:96, one launch (start us, length us, event | category | flops | bytes accessed | tf_op | source)
XLA Modules:
  0.0 185.7 jit_solution(13873036147186174615)
XLA Ops:
  0.8 2.4 %shard_map.119 = bf16[384,1664]{1,0:T(8,128)(2,1)S(1)} custom-call(s32[4]{0:T(128)S(1)} %pad_add_fusion.place_ref, bf16[3,256,512]{2,1,0:T(8,128)(2,1)} %inputs_ref.1, f32[1,512]{1,0:T(1,128)S(1)} %bitcast.131, bf16[512,1536]{1,0:T(8,128)(2,1)} %weight_ref.5), custom_call_target="tpu_custom_call" | custom-call | tf_op jit(solution)/shard_map/pallas_call | solution.py:86
  3.4 2.6 %shard_map.118 = bf16[480,1664]{1,0:T(8,128)(2,1)S(1)} custom-call(s32[4]{0:T(128)S(1)} %pad_add_fusion.place_ref, bf16[3,256,512]{2,1,0:T(8,128)(2,1)} %inputs_ref.1, f32[1,512]{1,0:T(1,128)S(1)} %bitcast.132, bf16[512,1536]{1,0:T(8,128)(2,1)} %weight_ref.5), custom_call_target="tpu_custom_call" | custom-call | tf_op jit(solution)/shard_map/pallas_call | solution.py:86
  6.5 3.2 %collective-permute-start.1 = (bf16[48,768]{1,0:T(8,128)(2,1)S(1)}, bf16[48,768]{1,0:T(8,128)(2,1)S(1)}, u32[]{:S(2)}, u32[]{:S(2)}) collective-permute-start(bf16[48,768]{1,0:T(8,128)(2,1)S(1)} %slice.323), channel_id=1, source_target_pairs={{0,32},{16,240},{32,64},{48,16},{64,96},{80,48},{96,128},{112,80},... | collective-permute-start | bytes 221192 | tf_op jit(solution)/shard_map/ppermute | solution.py:39
  11.8 3.7 %collective-permute-start.2 = (bf16[2,48,768]{2,1,0:T(8,128)(2,1)S(1)}, bf16[2,48,768]{2,1,0:T(8,128)(2,1)S(1)}, u32[]{:S(2)}, u32[]{:S(2)}) collective-permute-start(bf16[2,48,768]{2,1,0:T(8,128)(2,1)S(1)} %fusion.32), channel_id=1, source_target_pairs={{0,32},{16,240},{32,64},{48,16},{64,96},{80,48},{96,128},{112,80},... | collective-permute-start | bytes 442376 | tf_op jit(solution)/shard_map/ppermute | solution.py:39
  18.2 3.8 %collective-permute-start.3 = (bf16[2,48,768]{2,1,0:T(8,128)(2,1)S(1)}, bf16[2,48,768]{2,1,0:T(8,128)(2,1)S(1)}, u32[]{:S(2)}, u32[]{:S(2)}) collective-permute-start(bf16[2,48,768]{2,1,0:T(8,128)(2,1)S(1)} %fusion.33), channel_id=1, source_target_pairs={{0,32},{16,240},{32,64},{48,16},{64,96},{80,48},{96,128},{112,80},... | collective-permute-start | bytes 442376 | tf_op jit(solution)/shard_map/ppermute | solution.py:39
  24.7 3.8 %collective-permute-start.4 = (bf16[2,48,768]{2,1,0:T(8,128)(2,1)S(1)}, bf16[2,48,768]{2,1,0:T(8,128)(2,1)S(1)}, u32[]{:S(2)}, u32[]{:S(2)}) collective-permute-start(bf16[2,48,768]{2,1,0:T(8,128)(2,1)S(1)} %fusion.34), channel_id=1, source_target_pairs={{0,32},{16,240},{32,64},{48,16},{64,96},{80,48},{96,128},{112,80},... | collective-permute-start | bytes 442376 | tf_op jit(solution)/shard_map/ppermute | solution.py:39
  28.5 2.1 %collective-permute-start.8 = (bf16[2,48,896]{2,1,0:T(8,128)(2,1)S(1)}, bf16[2,48,896]{2,1,0:T(8,128)(2,1)S(1)}, u32[]{:S(2)}, u32[]{:S(2)}) collective-permute-start(bf16[2,48,896]{2,1,0:T(8,128)(2,1)S(1)} %fusion.29), channel_id=1, source_target_pairs={{0,32},{16,240},{32,64},{48,16},{64,96},{80,48},{96,128},{112,80},... | collective-permute-start | bytes 516104 | tf_op jit(solution)/shard_map/ppermute | solution.py:39
  31.3 2.7 %collective-permute-done.8 = bf16[2,48,896]{2,1,0:T(8,128)(2,1)S(1)} collective-permute-done((bf16[2,48,896]{2,1,0:T(8,128)(2,1)S(1)}, bf16[2,48,896]{2,1,0:T(8,128)(2,1)S(1)}, u32[]{:S(2)}, u32[]{:S(2)}) %collective-permute-start.8) | collective-permute-done | bytes 172064 | tf_op jit(solution)/shard_map/ppermute | solution.py:39
  35.5 4.6 %shard_map.120 = bf16[48,512]{1,0:T(8,128)(2,1)S(1)} custom-call(f32[4]{0:T(128)S(1)} %copy-done.6, f32[48,1664]{1,0:T(8,128)S(1)} %pad_maximum_fusion.6.ours_ref.our_sums_ref, f32[48,1664]{1,0:T(8,128)S(1)} %pad_maximum_fusion.6.ours_ref.our_sums_ref, bf16[48,1664]{1,0:T(8,128)(2,1)S(1)} %pad_maximum_fusion.8.theirs_ref.their_sums_ref, ...), custom_call_target="tpu_custom_call" | custom-call | tf_op jit(solution)/shard_map/pallas_call | solution.py:174
  40.1 18.3 %all_gather.3 = bf16[768,512]{1,0:T(8,128)(2,1)S(1)} all-gather(bf16[48,512]{1,0:T(8,128)(2,1)S(1)} %shard_map.120), channel_id=1, replica_groups=mesh['z'=8,'core'=2,'y'=4,'x'=4] {'z','core'}, dimensions={0}, use_global_device_ids=true | all-gather | bytes 835584 | tf_op jit(solution)/shard_map/all_gather | solution.py:295
  58.9 21.7 %all_to_all.15.partial_ref = bf16[16,48,512]{2,1,0:T(8,128)(2,1)S(1)} all-to-all(bf16[16,48,512]{2,1,0:T(8,128)(2,1)S(1)} %bitcast.148), channel_id=1, replica_groups=mesh['z'=8,'core'=2,'y'=4,'x'=4] {'y','x'}, dimensions={0} | all-to-all | bytes 1572864 | tf_op jit(solution)/shard_map/all_to_all | solution.py:298
  82.2 17.0 %all_to_all.16.rows_ref = bf16[16,48,512]{2,1,0:T(8,128)(2,1)S(1)} all-to-all(bf16[16,48,512]{2,1,0:T(8,128)(2,1)S(1)} %get-tuple-element.8), channel_id=1, replica_groups=mesh['z'=8,'core'=2,'y'=4,'x'=4] {'y','x'}, dimensions={0} | all-to-all | bytes 1572864 | tf_op jit(solution)/shard_map/all_to_all | solution.py:300
  108.8 2.9 %collective-permute-start.13 = (bf16[2,48,896]{2,1,0:T(8,128)(2,1)S(1)}, bf16[2,48,896]{2,1,0:T(8,128)(2,1)S(1)}, u32[]{:S(2)}, u32[]{:S(2)}) collective-permute-start(bf16[2,48,896]{2,1,0:T(8,128)(2,1)S(1)} %fusion.24), channel_id=1, source_target_pairs={{0,32},{16,240},{32,64},{48,16},{64,96},{80,48},{96,128},{112,80},... | collective-permute-start | bytes 516104 | tf_op jit(solution)/shard_map/ppermute | solution.py:39
  114.7 3.8 %collective-permute-start.14 = (bf16[2,48,896]{2,1,0:T(8,128)(2,1)S(1)}, bf16[2,48,896]{2,1,0:T(8,128)(2,1)S(1)}, u32[]{:S(2)}, u32[]{:S(2)}) collective-permute-start(bf16[2,48,896]{2,1,0:T(8,128)(2,1)S(1)} %fusion.25), channel_id=1, source_target_pairs={{0,32},{16,240},{32,64},{48,16},{64,96},{80,48},{96,128},{112,80},... | collective-permute-start | bytes 516104 | tf_op jit(solution)/shard_map/ppermute | solution.py:39
  121.4 3.8 %collective-permute-start.15 = (bf16[2,48,896]{2,1,0:T(8,128)(2,1)S(1)}, bf16[2,48,896]{2,1,0:T(8,128)(2,1)S(1)}, u32[]{:S(2)}, u32[]{:S(2)}) collective-permute-start(bf16[2,48,896]{2,1,0:T(8,128)(2,1)S(1)} %fusion.26), channel_id=1, source_target_pairs={{0,32},{16,240},{32,64},{48,16},{64,96},{80,48},{96,128},{112,80},... | collective-permute-start | bytes 516104 | tf_op jit(solution)/shard_map/ppermute | solution.py:39
  125.2 2.3 %collective-permute-start.19 = (bf16[2,48,1024]{2,1,0:T(8,128)(2,1)S(1)}, bf16[2,48,1024]{2,1,0:T(8,128)(2,1)S(1)}, u32[]{:S(2)}, u32[]{:S(2)}) collective-permute-start(bf16[2,48,1024]{2,1,0:T(8,128)(2,1)S(1)} %fusion.22), channel_id=1, source_target_pairs={{0,32},{16,240},{32,64},{48,16},{64,96},{80,48},{96,128},{112,80},... | collective-permute-start | bytes 589832 | tf_op jit(solution)/shard_map/ppermute | solution.py:39
  128.3 2.7 %collective-permute-done.19 = bf16[2,48,1024]{2,1,0:T(8,128)(2,1)S(1)} collective-permute-done((bf16[2,48,1024]{2,1,0:T(8,128)(2,1)S(1)}, bf16[2,48,1024]{2,1,0:T(8,128)(2,1)S(1)}, u32[]{:S(2)}, u32[]{:S(2)}) %collective-permute-start.19) | collective-permute-done | bytes 196640 | tf_op jit(solution)/shard_map/ppermute | solution.py:39
  134.4 3.8 %collective-permute-start.25 = (bf16[2,48,896]{2,1,0:T(8,128)(2,1)S(1)}, bf16[2,48,896]{2,1,0:T(8,128)(2,1)S(1)}, u32[]{:S(2)}, u32[]{:S(2)}) collective-permute-start(bf16[2,48,896]{2,1,0:T(8,128)(2,1)S(1)} %get-tuple-element.25), channel_id=1, source_target_pairs={{0,32},{16,240},{32,64},{48,16},{64,96},{80,48},{96,128},{112,80},... | collective-permute-start | bytes 516104 | tf_op jit(solution)/shard_map/ppermute | solution.py:39
  138.5 2.5 %collective-permute-done.25 = bf16[2,48,896]{2,1,0:T(8,128)(2,1)S(1)} collective-permute-done((bf16[2,48,896]{2,1,0:T(8,128)(2,1)S(1)}, bf16[2,48,896]{2,1,0:T(8,128)(2,1)S(1)}, u32[]{:S(2)}, u32[]{:S(2)}) %collective-permute-start.25) | collective-permute-done | bytes 172064 | tf_op jit(solution)/shard_map/ppermute | solution.py:39
  141.5 3.8 %collective-permute-start.29 = (bf16[2,48,896]{2,1,0:T(8,128)(2,1)S(1)}, bf16[2,48,896]{2,1,0:T(8,128)(2,1)S(1)}, u32[]{:S(2)}, u32[]{:S(2)}) collective-permute-start(bf16[2,48,896]{2,1,0:T(8,128)(2,1)S(1)} %collective-permute-done.25), channel_id=1, source_target_pairs={{0,32},{16,240},{32,64},{48,16},{64,96},{80,48},{96,128},{112,80},... | collective-permute-start | bytes 516104 | tf_op jit(solution)/shard_map/ppermute | solution.py:39
  148.4 2.2 %collective-permute-done.27 = bf16[2,48,896]{2,1,0:T(8,128)(2,1)S(1)} collective-permute-done((bf16[2,48,896]{2,1,0:T(8,128)(2,1)S(1)}, bf16[2,48,896]{2,1,0:T(8,128)(2,1)S(1)}, u32[]{:S(2)}, u32[]{:S(2)}) %collective-permute-start.27) | collective-permute-done | bytes 172064 | tf_op jit(solution)/shard_map/ppermute | solution.py:39
  150.6 3.0 %collective-permute-start.31 = (bf16[2,48,896]{2,1,0:T(8,128)(2,1)S(1)}, bf16[2,48,896]{2,1,0:T(8,128)(2,1)S(1)}, u32[]{:S(2)}, u32[]{:S(2)}) collective-permute-start(bf16[2,48,896]{2,1,0:T(8,128)(2,1)S(1)} %collective-permute-done.27), channel_id=1, source_target_pairs={{0,32},{16,240},{32,64},{48,16},{64,96},{80,48},{96,128},{112,80},... | collective-permute-start | bytes 516104 | tf_op jit(solution)/shard_map/ppermute | solution.py:39
  156.6 3.7 %collective-permute-start.35 = (bf16[2,48,896]{2,1,0:T(8,128)(2,1)S(1)}, bf16[2,48,896]{2,1,0:T(8,128)(2,1)S(1)}, u32[]{:S(2)}, u32[]{:S(2)}) collective-permute-start(bf16[2,48,896]{2,1,0:T(8,128)(2,1)S(1)} %collective-permute-done.31), channel_id=1, source_target_pairs={{0,32},{16,240},{32,64},{48,16},{64,96},{80,48},{96,128},{112,80},... | collective-permute-start | bytes 516104 | tf_op jit(solution)/shard_map/ppermute | solution.py:39
  166.9 18.0 %all_to_all.17 = bf16[16,48,512]{2,1,0:T(8,128)(2,1)S(1)} all-to-all(bf16[16,48,512]{2,1,0:T(8,128)(2,1)S(1)} %bitcast.134), channel_id=1, replica_groups=mesh['z'=8,'core'=2,'y'=4,'x'=4] {'y','x'}, dimensions={0} | all-to-all | bytes 1572864 | tf_op jit(solution)/shard_map/all_to_all | solution.py:309
  (161 shorter events, 46.8 us)
Async XLA Ops:
  9.7 5.8 %collective-permute-start.5 = (bf16[48,896]{1,0:T(8,128)(2,1)S(1)}, bf16[48,896]{1,0:T(8,128)(2,1)S(1)}, u32[]{:S(2)}, u32[]{:S(2)}) collective-permute-start(bf16[48,896]{1,0:T(8,128)(2,1)S(1)} %slice.330), channel_id=1, source_target_pairs={{0,32},{16,240},{32,64},{48,16},{64,96},{80,48},{96,128},{112,80},... | collective-permute-start | bytes 258056 | tf_op jit(solution)/shard_map/ppermute | solution.py:39
  11.8 6.3 %collective-permute-start.2 = (bf16[2,48,768]{2,1,0:T(8,128)(2,1)S(1)}, bf16[2,48,768]{2,1,0:T(8,128)(2,1)S(1)}, u32[]{:S(2)}, u32[]{:S(2)}) collective-permute-start(bf16[2,48,768]{2,1,0:T(8,128)(2,1)S(1)} %fusion.32), channel_id=1, source_target_pairs={{0,32},{16,240},{32,64},{48,16},{64,96},{80,48},{96,128},{112,80},... | collective-permute-start | bytes 442376 | tf_op jit(solution)/shard_map/ppermute | solution.py:39
  15.6 6.3 %collective-permute-start.6 = (bf16[2,48,896]{2,1,0:T(8,128)(2,1)S(1)}, bf16[2,48,896]{2,1,0:T(8,128)(2,1)S(1)}, u32[]{:S(2)}, u32[]{:S(2)}) collective-permute-start(bf16[2,48,896]{2,1,0:T(8,128)(2,1)S(1)} %fusion.27), channel_id=1, source_target_pairs={{0,32},{16,240},{32,64},{48,16},{64,96},{80,48},{96,128},{112,80},... | collective-permute-start | bytes 516104 | tf_op jit(solution)/shard_map/ppermute | solution.py:39
  18.2 6.4 %collective-permute-start.3 = (bf16[2,48,768]{2,1,0:T(8,128)(2,1)S(1)}, bf16[2,48,768]{2,1,0:T(8,128)(2,1)S(1)}, u32[]{:S(2)}, u32[]{:S(2)}) collective-permute-start(bf16[2,48,768]{2,1,0:T(8,128)(2,1)S(1)} %fusion.33), channel_id=1, source_target_pairs={{0,32},{16,240},{32,64},{48,16},{64,96},{80,48},{96,128},{112,80},... | collective-permute-start | bytes 442376 | tf_op jit(solution)/shard_map/ppermute | solution.py:39
  22.0 6.4 %collective-permute-start.7 = (bf16[2,48,896]{2,1,0:T(8,128)(2,1)S(1)}, bf16[2,48,896]{2,1,0:T(8,128)(2,1)S(1)}, u32[]{:S(2)}, u32[]{:S(2)}) collective-permute-start(bf16[2,48,896]{2,1,0:T(8,128)(2,1)S(1)} %fusion.28), channel_id=1, source_target_pairs={{0,32},{16,240},{32,64},{48,16},{64,96},{80,48},{96,128},{112,80},... | collective-permute-start | bytes 516104 | tf_op jit(solution)/shard_map/ppermute | solution.py:39
  24.7 6.4 %collective-permute-start.4 = (bf16[2,48,768]{2,1,0:T(8,128)(2,1)S(1)}, bf16[2,48,768]{2,1,0:T(8,128)(2,1)S(1)}, u32[]{:S(2)}, u32[]{:S(2)}) collective-permute-start(bf16[2,48,768]{2,1,0:T(8,128)(2,1)S(1)} %fusion.34), channel_id=1, source_target_pairs={{0,32},{16,240},{32,64},{48,16},{64,96},{80,48},{96,128},{112,80},... | collective-permute-start | bytes 442376 | tf_op jit(solution)/shard_map/ppermute | solution.py:39
  28.5 5.5 %collective-permute-start.8 = (bf16[2,48,896]{2,1,0:T(8,128)(2,1)S(1)}, bf16[2,48,896]{2,1,0:T(8,128)(2,1)S(1)}, u32[]{:S(2)}, u32[]{:S(2)}) collective-permute-start(bf16[2,48,896]{2,1,0:T(8,128)(2,1)S(1)} %fusion.29), channel_id=1, source_target_pairs={{0,32},{16,240},{32,64},{48,16},{64,96},{80,48},{96,128},{112,80},... | collective-permute-start | bytes 516104 | tf_op jit(solution)/shard_map/ppermute | solution.py:39
  105.8 5.9 %collective-permute-start.16 = (bf16[48,1024]{1,0:T(8,128)(2,1)S(1)}, bf16[48,1024]{1,0:T(8,128)(2,1)S(1)}, u32[]{:S(2)}, u32[]{:S(2)}) collective-permute-start(bf16[48,1024]{1,0:T(8,128)(2,1)S(1)} %slice.355), channel_id=1, source_target_pairs={{0,32},{16,240},{32,64},{48,16},{64,96},{80,48},{96,128},{112,80},... | collective-permute-start | bytes 294920 | tf_op jit(solution)/shard_map/ppermute | solution.py:39
  108.8 5.8 %collective-permute-start.13 = (bf16[2,48,896]{2,1,0:T(8,128)(2,1)S(1)}, bf16[2,48,896]{2,1,0:T(8,128)(2,1)S(1)}, u32[]{:S(2)}, u32[]{:S(2)}) collective-permute-start(bf16[2,48,896]{2,1,0:T(8,128)(2,1)S(1)} %fusion.24), channel_id=1, source_target_pairs={{0,32},{16,240},{32,64},{48,16},{64,96},{80,48},{96,128},{112,80},... | collective-permute-start | bytes 516104 | tf_op jit(solution)/shard_map/ppermute | solution.py:39
  111.8 6.6 %collective-permute-start.17 = (bf16[2,48,1024]{2,1,0:T(8,128)(2,1)S(1)}, bf16[2,48,1024]{2,1,0:T(8,128)(2,1)S(1)}, u32[]{:S(2)}, u32[]{:S(2)}) collective-permute-start(bf16[2,48,1024]{2,1,0:T(8,128)(2,1)S(1)} %fusion.20), channel_id=1, source_target_pairs={{0,32},{16,240},{32,64},{48,16},{64,96},{80,48},{96,128},{112,80},... | collective-permute-start | bytes 589832 | tf_op jit(solution)/shard_map/ppermute | solution.py:39
  114.7 6.7 %collective-permute-start.14 = (bf16[2,48,896]{2,1,0:T(8,128)(2,1)S(1)}, bf16[2,48,896]{2,1,0:T(8,128)(2,1)S(1)}, u32[]{:S(2)}, u32[]{:S(2)}) collective-permute-start(bf16[2,48,896]{2,1,0:T(8,128)(2,1)S(1)} %fusion.25), channel_id=1, source_target_pairs={{0,32},{16,240},{32,64},{48,16},{64,96},{80,48},{96,128},{112,80},... | collective-permute-start | bytes 516104 | tf_op jit(solution)/shard_map/ppermute | solution.py:39
  118.5 6.7 %collective-permute-start.18 = (bf16[2,48,1024]{2,1,0:T(8,128)(2,1)S(1)}, bf16[2,48,1024]{2,1,0:T(8,128)(2,1)S(1)}, u32[]{:S(2)}, u32[]{:S(2)}) collective-permute-start(bf16[2,48,1024]{2,1,0:T(8,128)(2,1)S(1)} %fusion.21), channel_id=1, source_target_pairs={{0,32},{16,240},{32,64},{48,16},{64,96},{80,48},{96,128},{112,80},... | collective-permute-start | bytes 589832 | tf_op jit(solution)/shard_map/ppermute | solution.py:39
  121.4 6.7 %collective-permute-start.15 = (bf16[2,48,896]{2,1,0:T(8,128)(2,1)S(1)}, bf16[2,48,896]{2,1,0:T(8,128)(2,1)S(1)}, u32[]{:S(2)}, u32[]{:S(2)}) collective-permute-start(bf16[2,48,896]{2,1,0:T(8,128)(2,1)S(1)} %fusion.26), channel_id=1, source_target_pairs={{0,32},{16,240},{32,64},{48,16},{64,96},{80,48},{96,128},{112,80},... | collective-permute-start | bytes 516104 | tf_op jit(solution)/shard_map/ppermute | solution.py:39
  125.2 5.7 %collective-permute-start.19 = (bf16[2,48,1024]{2,1,0:T(8,128)(2,1)S(1)}, bf16[2,48,1024]{2,1,0:T(8,128)(2,1)S(1)}, u32[]{:S(2)}, u32[]{:S(2)}) collective-permute-start(bf16[2,48,1024]{2,1,0:T(8,128)(2,1)S(1)} %fusion.22), channel_id=1, source_target_pairs={{0,32},{16,240},{32,64},{48,16},{64,96},{80,48},{96,128},{112,80},... | collective-permute-start | bytes 589832 | tf_op jit(solution)/shard_map/ppermute | solution.py:39
  134.4 6.7 %collective-permute-start.25 = (bf16[2,48,896]{2,1,0:T(8,128)(2,1)S(1)}, bf16[2,48,896]{2,1,0:T(8,128)(2,1)S(1)}, u32[]{:S(2)}, u32[]{:S(2)}) collective-permute-start(bf16[2,48,896]{2,1,0:T(8,128)(2,1)S(1)} %get-tuple-element.25), channel_id=1, source_target_pairs={{0,32},{16,240},{32,64},{48,16},{64,96},{80,48},{96,128},{112,80},... | collective-permute-start | bytes 516104 | tf_op jit(solution)/shard_map/ppermute | solution.py:39
  138.1 7.1 %collective-permute-start.23 = (bf16[2,48,896]{2,1,0:T(8,128)(2,1)S(1)}, bf16[2,48,896]{2,1,0:T(8,128)(2,1)S(1)}, u32[]{:S(2)}, u32[]{:S(2)}) collective-permute-start(bf16[2,48,896]{2,1,0:T(8,128)(2,1)S(1)} %get-tuple-element.26), channel_id=1, source_target_pairs={{0,32},{16,240},{32,64},{48,16},{64,96},{80,48},{96,128},{112,80},... | collective-permute-start | bytes 516104 | tf_op jit(solution)/shard_map/ppermute | solution.py:39
  141.1 5.5 %collective-permute-start.26 = (bf16[2,48,896]{2,1,0:T(8,128)(2,1)S(1)}, bf16[2,48,896]{2,1,0:T(8,128)(2,1)S(1)}, u32[]{:S(2)}, u32[]{:S(2)}) collective-permute-start(bf16[2,48,896]{2,1,0:T(8,128)(2,1)S(1)} %collective-permute-done.25), channel_id=1, source_target_pairs={{0,16},{16,0},{1,17},{17,1},{2,18},{18,2},{3,19},{19,3},{4,20},{20... | collective-permute-start | bytes 516104 | tf_op jit(solution)/shard_map/ppermute | solution.py:30
  141.5 12.3 %collective-permute-start.29 = (bf16[2,48,896]{2,1,0:T(8,128)(2,1)S(1)}, bf16[2,48,896]{2,1,0:T(8,128)(2,1)S(1)}, u32[]{:S(2)}, u32[]{:S(2)}) collective-permute-start(bf16[2,48,896]{2,1,0:T(8,128)(2,1)S(1)} %collective-permute-done.25), channel_id=1, source_target_pairs={{0,32},{16,240},{32,64},{48,16},{64,96},{80,48},{96,128},{112,80},... | collective-permute-start | bytes 516104 | tf_op jit(solution)/shard_map/ppermute | solution.py:39
  145.2 5.4 %collective-permute-start.27 = (bf16[2,48,896]{2,1,0:T(8,128)(2,1)S(1)}, bf16[2,48,896]{2,1,0:T(8,128)(2,1)S(1)}, u32[]{:S(2)}, u32[]{:S(2)}) collective-permute-start(bf16[2,48,896]{2,1,0:T(8,128)(2,1)S(1)} %collective-permute-done.23), channel_id=1, source_target_pairs={{0,32},{16,240},{32,64},{48,16},{64,96},{80,48},{96,128},{112,80},... | collective-permute-start | bytes 516104 | tf_op jit(solution)/shard_map/ppermute | solution.py:39
  150.6 6.0 %collective-permute-start.31 = (bf16[2,48,896]{2,1,0:T(8,128)(2,1)S(1)}, bf16[2,48,896]{2,1,0:T(8,128)(2,1)S(1)}, u32[]{:S(2)}, u32[]{:S(2)}) collective-permute-start(bf16[2,48,896]{2,1,0:T(8,128)(2,1)S(1)} %collective-permute-done.27), channel_id=1, source_target_pairs={{0,32},{16,240},{32,64},{48,16},{64,96},{80,48},{96,128},{112,80},... | collective-permute-start | bytes 516104 | tf_op jit(solution)/shard_map/ppermute | solution.py:39
  153.7 6.6 %collective-permute-start.33 = (bf16[2,48,896]{2,1,0:T(8,128)(2,1)S(1)}, bf16[2,48,896]{2,1,0:T(8,128)(2,1)S(1)}, u32[]{:S(2)}, u32[]{:S(2)}) collective-permute-start(bf16[2,48,896]{2,1,0:T(8,128)(2,1)S(1)} %collective-permute-done.29), channel_id=1, source_target_pairs={{0,32},{16,240},{32,64},{48,16},{64,96},{80,48},{96,128},{112,80},... | collective-permute-start | bytes 516104 | tf_op jit(solution)/shard_map/ppermute | solution.py:39
  156.6 10.0 %collective-permute-start.35 = (bf16[2,48,896]{2,1,0:T(8,128)(2,1)S(1)}, bf16[2,48,896]{2,1,0:T(8,128)(2,1)S(1)}, u32[]{:S(2)}, u32[]{:S(2)}) collective-permute-start(bf16[2,48,896]{2,1,0:T(8,128)(2,1)S(1)} %collective-permute-done.31), channel_id=1, source_target_pairs={{0,32},{16,240},{32,64},{48,16},{64,96},{80,48},{96,128},{112,80},... | collective-permute-start | bytes 516104 | tf_op jit(solution)/shard_map/ppermute | solution.py:39
  160.3 5.8 %collective-permute-start.32 = (bf16[2,48,896]{2,1,0:T(8,128)(2,1)S(1)}, bf16[2,48,896]{2,1,0:T(8,128)(2,1)S(1)}, u32[]{:S(2)}, u32[]{:S(2)}) collective-permute-start(bf16[2,48,896]{2,1,0:T(8,128)(2,1)S(1)} %collective-permute-done.31), channel_id=1, source_target_pairs={{0,16},{16,0},{1,17},{17,1},{2,18},{18,2},{3,19},{19,3},{4,20},{20... | collective-permute-start | bytes 516104 | tf_op jit(solution)/shard_map/ppermute | solution.py:30
  160.3 5.5 %collective-permute-start.36 = (bf16[2,48,896]{2,1,0:T(8,128)(2,1)S(1)}, bf16[2,48,896]{2,1,0:T(8,128)(2,1)S(1)}, u32[]{:S(2)}, u32[]{:S(2)}) collective-permute-start(bf16[2,48,896]{2,1,0:T(8,128)(2,1)S(1)} %collective-permute-done.33), channel_id=1, source_target_pairs={{0,32},{16,240},{32,64},{48,16},{64,96},{80,48},{96,128},{112,80},... | collective-permute-start | bytes 516104 | tf_op jit(solution)/shard_map/ppermute | solution.py:39
  (22 other events, 164.1 us)

commit v3 on v2

--- a/solution.py
+++ b/solution.py
@@ -69,7 +69,7 @@
                     values = block.astype(jnp.float32) * gain
                 squares = jnp.sum(values * values, axis=-1, keepdims=True)
                 out_ref[at : at + share, width:] = pieces_of(squares, source).astype(out_ref.dtype)
-    chunk = 256
+    chunk = width // 2
     for at in range(0, width, chunk):
         out_ref[:, at : at + chunk] = jnp.dot(
             picked_ref[...], weight_ref[:, at : at + chunk], preferred_element_type=jnp.float32

time: 186 us -> 186 us (level)
  no operation moved by 1% of the time
where the time goes in v3:
time: 186 us
  blocking collectives  74.9 us (40%)
  starting transfers between devices  59.1 us (32%)
  waiting for transfers between devices  27.8 us (15%)
  Pallas kernels  14.5 us (8%)
  matrix products  3.92 us (2%)
  other arithmetic  3.82 us (2%)
    ppermute x24, starting transfers between devices, pass_on(): return lax.ppermute(value, BATCH, pairs)  57.5 us
    all_to_all x1, blocking collectives, on_device(): partial = lax.all_to_all(partial, TENSOR, 0, 0, tiled=True)  21.7 us
    ppermute x24, waiting for transfers between devices, pass_on(): return lax.ppermute(value, BATCH, pairs)  19.3 us
    all_gather x1, blocking collectives, on_device(): everyone = lax.all_gather(spiked, BATCH, axis=0, tiled=True)  18.3 us
    all_to_all x1, blocking collectives, on_device(): lax.all_to_all(partial.reshape(blocks, each, features), TENSOR, 0, 0, til...  18 us
    all_to_all x1, blocking collectives, on_device(): hidden = lax.all_to_all(hidden, TENSOR, 0, 0, tiled=True)  17 us
    ppermute x13, waiting for transfers between devices, swap_cores(): return lax.ppermute(value, 'core', [(0, 1), (1, 0)])  8.47 us
    pallas_call x4, Pallas kernels, product(): pl.pallas_call(functools.partial(product_kernel, chips, first, which), in...  8.44 us
  transfers between devices with their start and end apart: 37, of which 22 were waited for; matrix products, arithmetic and copies ran while one was open for 3% of the time, Pallas kernels for 2%

profile of v3, /device:TPU:96, one launch (start us, length us, event | category | flops | bytes accessed | tf_op | source)
XLA Modules:
  0.0 185.8 jit_solution(4602498718920815906)
XLA Ops:
  0.8 2.4 %shard_map.119 = bf16[384,1664]{1,0:T(8,128)(2,1)S(1)} custom-call(s32[4]{0:T(128)S(1)} %pad_add_fusion.place_ref, bf16[3,256,512]{2,1,0:T(8,128)(2,1)} %inputs_ref.1, f32[1,512]{1,0:T(1,128)S(1)} %bitcast.131, bf16[512,1536]{1,0:T(8,128)(2,1)} %weight_ref.5), custom_call_target="tpu_custom_call" | custom-call | tf_op jit(solution)/shard_map/pallas_call | solution.py:86
  3.4 2.6 %shard_map.118 = bf16[480,1664]{1,0:T(8,128)(2,1)S(1)} custom-call(s32[4]{0:T(128)S(1)} %pad_add_fusion.place_ref, bf16[3,256,512]{2,1,0:T(8,128)(2,1)} %inputs_ref.1, f32[1,512]{1,0:T(1,128)S(1)} %bitcast.132, bf16[512,1536]{1,0:T(8,128)(2,1)} %weight_ref.5), custom_call_target="tpu_custom_call" | custom-call | tf_op jit(solution)/shard_map/pallas_call | solution.py:86
  6.5 3.2 %collective-permute-start.1 = (bf16[48,768]{1,0:T(8,128)(2,1)S(1)}, bf16[48,768]{1,0:T(8,128)(2,1)S(1)}, u32[]{:S(2)}, u32[]{:S(2)}) collective-permute-start(bf16[48,768]{1,0:T(8,128)(2,1)S(1)} %slice.323), channel_id=1, source_target_pairs={{0,32},{16,240},{32,64},{48,16},{64,96},{80,48},{96,128},{112,80},... | collective-permute-start | bytes 221192 | tf_op jit(solution)/shard_map/ppermute | solution.py:39
  11.8 3.7 %collective-permute-start.2 = (bf16[2,48,768]{2,1,0:T(8,128)(2,1)S(1)}, bf16[2,48,768]{2,1,0:T(8,128)(2,1)S(1)}, u32[]{:S(2)}, u32[]{:S(2)}) collective-permute-start(bf16[2,48,768]{2,1,0:T(8,128)(2,1)S(1)} %fusion.32), channel_id=1, source_target_pairs={{0,32},{16,240},{32,64},{48,16},{64,96},{80,48},{96,128},{112,80},... | collective-permute-start | bytes 442376 | tf_op jit(solution)/shard_map/ppermute | solution.py:39
  18.2 3.8 %collective-permute-start.3 = (bf16[2,48,768]{2,1,0:T(8,128)(2,1)S(1)}, bf16[2,48,768]{2,1,0:T(8,128)(2,1)S(1)}, u32[]{:S(2)}, u32[]{:S(2)}) collective-permute-start(bf16[2,48,768]{2,1,0:T(8,128)(2,1)S(1)} %fusion.33), channel_id=1, source_target_pairs={{0,32},{16,240},{32,64},{48,16},{64,96},{80,48},{96,128},{112,80},... | collective-permute-start | bytes 442376 | tf_op jit(solution)/shard_map/ppermute | solution.py:39
  24.7 3.8 %collective-permute-start.4 = (bf16[2,48,768]{2,1,0:T(8,128)(2,1)S(1)}, bf16[2,48,768]{2,1,0:T(8,128)(2,1)S(1)}, u32[]{:S(2)}, u32[]{:S(2)}) collective-permute-start(bf16[2,48,768]{2,1,0:T(8,128)(2,1)S(1)} %fusion.34), channel_id=1, source_target_pairs={{0,32},{16,240},{32,64},{48,16},{64,96},{80,48},{96,128},{112,80},... | collective-permute-start | bytes 442376 | tf_op jit(solution)/shard_map/ppermute | solution.py:39
  28.5 2.1 %collective-permute-start.8 = (bf16[2,48,896]{2,1,0:T(8,128)(2,1)S(1)}, bf16[2,48,896]{2,1,0:T(8,128)(2,1)S(1)}, u32[]{:S(2)}, u32[]{:S(2)}) collective-permute-start(bf16[2,48,896]{2,1,0:T(8,128)(2,1)S(1)} %fusion.29), channel_id=1, source_target_pairs={{0,32},{16,240},{32,64},{48,16},{64,96},{80,48},{96,128},{112,80},... | collective-permute-start | bytes 516104 | tf_op jit(solution)/shard_map/ppermute | solution.py:39
  31.3 2.7 %collective-permute-done.8 = bf16[2,48,896]{2,1,0:T(8,128)(2,1)S(1)} collective-permute-done((bf16[2,48,896]{2,1,0:T(8,128)(2,1)S(1)}, bf16[2,48,896]{2,1,0:T(8,128)(2,1)S(1)}, u32[]{:S(2)}, u32[]{:S(2)}) %collective-permute-start.8) | collective-permute-done | bytes 172064 | tf_op jit(solution)/shard_map/ppermute | solution.py:39
  35.5 4.6 %shard_map.120 = bf16[48,512]{1,0:T(8,128)(2,1)S(1)} custom-call(f32[4]{0:T(128)S(1)} %copy-done.6, f32[48,1664]{1,0:T(8,128)S(1)} %pad_maximum_fusion.6.ours_ref.our_sums_ref, f32[48,1664]{1,0:T(8,128)S(1)} %pad_maximum_fusion.6.ours_ref.our_sums_ref, bf16[48,1664]{1,0:T(8,128)(2,1)S(1)} %pad_maximum_fusion.8.theirs_ref.their_sums_ref, ...), custom_call_target="tpu_custom_call" | custom-call | tf_op jit(solution)/shard_map/pallas_call | solution.py:174
  40.1 18.3 %all_gather.3 = bf16[768,512]{1,0:T(8,128)(2,1)S(1)} all-gather(bf16[48,512]{1,0:T(8,128)(2,1)S(1)} %shard_map.120), channel_id=1, replica_groups=mesh['z'=8,'core'=2,'y'=4,'x'=4] {'z','core'}, dimensions={0}, use_global_device_ids=true | all-gather | bytes 835584 | tf_op jit(solution)/shard_map/all_gather | solution.py:295
  58.9 21.7 %all_to_all.15.partial_ref = bf16[16,48,512]{2,1,0:T(8,128)(2,1)S(1)} all-to-all(bf16[16,48,512]{2,1,0:T(8,128)(2,1)S(1)} %bitcast.148), channel_id=1, replica_groups=mesh['z'=8,'core'=2,'y'=4,'x'=4] {'y','x'}, dimensions={0} | all-to-all | bytes 1572864 | tf_op jit(solution)/shard_map/all_to_all | solution.py:298
  82.2 17.0 %all_to_all.16.rows_ref = bf16[16,48,512]{2,1,0:T(8,128)(2,1)S(1)} all-to-all(bf16[16,48,512]{2,1,0:T(8,128)(2,1)S(1)} %get-tuple-element.8), channel_id=1, replica_groups=mesh['z'=8,'core'=2,'y'=4,'x'=4] {'y','x'}, dimensions={0} | all-to-all | bytes 1572864 | tf_op jit(solution)/shard_map/all_to_all | solution.py:300
  108.9 2.9 %collective-permute-start.13 = (bf16[2,48,896]{2,1,0:T(8,128)(2,1)S(1)}, bf16[2,48,896]{2,1,0:T(8,128)(2,1)S(1)}, u32[]{:S(2)}, u32[]{:S(2)}) collective-permute-start(bf16[2,48,896]{2,1,0:T(8,128)(2,1)S(1)} %fusion.24), channel_id=1, source_target_pairs={{0,32},{16,240},{32,64},{48,16},{64,96},{80,48},{96,128},{112,80},... | collective-permute-start | bytes 516104 | tf_op jit(solution)/shard_map/ppermute | solution.py:39
  114.8 3.8 %collective-permute-start.14 = (bf16[2,48,896]{2,1,0:T(8,128)(2,1)S(1)}, bf16[2,48,896]{2,1,0:T(8,128)(2,1)S(1)}, u32[]{:S(2)}, u32[]{:S(2)}) collective-permute-start(bf16[2,48,896]{2,1,0:T(8,128)(2,1)S(1)} %fusion.25), channel_id=1, source_target_pairs={{0,32},{16,240},{32,64},{48,16},{64,96},{80,48},{96,128},{112,80},... | collective-permute-start | bytes 516104 | tf_op jit(solution)/shard_map/ppermute | solution.py:39
  121.5 3.8 %collective-permute-start.15 = (bf16[2,48,896]{2,1,0:T(8,128)(2,1)S(1)}, bf16[2,48,896]{2,1,0:T(8,128)(2,1)S(1)}, u32[]{:S(2)}, u32[]{:S(2)}) collective-permute-start(bf16[2,48,896]{2,1,0:T(8,128)(2,1)S(1)} %fusion.26), channel_id=1, source_target_pairs={{0,32},{16,240},{32,64},{48,16},{64,96},{80,48},{96,128},{112,80},... | collective-permute-start | bytes 516104 | tf_op jit(solution)/shard_map/ppermute | solution.py:39
  125.3 2.3 %collective-permute-start.19 = (bf16[2,48,1024]{2,1,0:T(8,128)(2,1)S(1)}, bf16[2,48,1024]{2,1,0:T(8,128)(2,1)S(1)}, u32[]{:S(2)}, u32[]{:S(2)}) collective-permute-start(bf16[2,48,1024]{2,1,0:T(8,128)(2,1)S(1)} %fusion.22), channel_id=1, source_target_pairs={{0,32},{16,240},{32,64},{48,16},{64,96},{80,48},{96,128},{112,80},... | collective-permute-start | bytes 589832 | tf_op jit(solution)/shard_map/ppermute | solution.py:39
  128.4 2.7 %collective-permute-done.19 = bf16[2,48,1024]{2,1,0:T(8,128)(2,1)S(1)} collective-permute-done((bf16[2,48,1024]{2,1,0:T(8,128)(2,1)S(1)}, bf16[2,48,1024]{2,1,0:T(8,128)(2,1)S(1)}, u32[]{:S(2)}, u32[]{:S(2)}) %collective-permute-start.19) | collective-permute-done | bytes 196640 | tf_op jit(solution)/shard_map/ppermute | solution.py:39
  134.7 3.5 %collective-permute-start.25 = (bf16[2,48,896]{2,1,0:T(8,128)(2,1)S(1)}, bf16[2,48,896]{2,1,0:T(8,128)(2,1)S(1)}, u32[]{:S(2)}, u32[]{:S(2)}) collective-permute-start(bf16[2,48,896]{2,1,0:T(8,128)(2,1)S(1)} %get-tuple-element.25), channel_id=1, source_target_pairs={{0,32},{16,240},{32,64},{48,16},{64,96},{80,48},{96,128},{112,80},... | collective-permute-start | bytes 516104 | tf_op jit(solution)/shard_map/ppermute | solution.py:39
  138.6 2.5 %collective-permute-done.25 = bf16[2,48,896]{2,1,0:T(8,128)(2,1)S(1)} collective-permute-done((bf16[2,48,896]{2,1,0:T(8,128)(2,1)S(1)}, bf16[2,48,896]{2,1,0:T(8,128)(2,1)S(1)}, u32[]{:S(2)}, u32[]{:S(2)}) %collective-permute-start.25) | collective-permute-done | bytes 172064 | tf_op jit(solution)/shard_map/ppermute | solution.py:39
  141.6 3.8 %collective-permute-start.29 = (bf16[2,48,896]{2,1,0:T(8,128)(2,1)S(1)}, bf16[2,48,896]{2,1,0:T(8,128)(2,1)S(1)}, u32[]{:S(2)}, u32[]{:S(2)}) collective-permute-start(bf16[2,48,896]{2,1,0:T(8,128)(2,1)S(1)} %collective-permute-done.25), channel_id=1, source_target_pairs={{0,32},{16,240},{32,64},{48,16},{64,96},{80,48},{96,128},{112,80},... | collective-permute-start | bytes 516104 | tf_op jit(solution)/shard_map/ppermute | solution.py:39
  148.5 2.2 %collective-permute-done.27 = bf16[2,48,896]{2,1,0:T(8,128)(2,1)S(1)} collective-permute-done((bf16[2,48,896]{2,1,0:T(8,128)(2,1)S(1)}, bf16[2,48,896]{2,1,0:T(8,128)(2,1)S(1)}, u32[]{:S(2)}, u32[]{:S(2)}) %collective-permute-start.27) | collective-permute-done | bytes 172064 | tf_op jit(solution)/shard_map/ppermute | solution.py:39
  150.7 3.0 %collective-permute-start.31 = (bf16[2,48,896]{2,1,0:T(8,128)(2,1)S(1)}, bf16[2,48,896]{2,1,0:T(8,128)(2,1)S(1)}, u32[]{:S(2)}, u32[]{:S(2)}) collective-permute-start(bf16[2,48,896]{2,1,0:T(8,128)(2,1)S(1)} %collective-permute-done.27), channel_id=1, source_target_pairs={{0,32},{16,240},{32,64},{48,16},{64,96},{80,48},{96,128},{112,80},... | collective-permute-start | bytes 516104 | tf_op jit(solution)/shard_map/ppermute | solution.py:39
  156.7 3.7 %collective-permute-start.35 = (bf16[2,48,896]{2,1,0:T(8,128)(2,1)S(1)}, bf16[2,48,896]{2,1,0:T(8,128)(2,1)S(1)}, u32[]{:S(2)}, u32[]{:S(2)}) collective-permute-start(bf16[2,48,896]{2,1,0:T(8,128)(2,1)S(1)} %collective-permute-done.31), channel_id=1, source_target_pairs={{0,32},{16,240},{32,64},{48,16},{64,96},{80,48},{96,128},{112,80},... | collective-permute-start | bytes 516104 | tf_op jit(solution)/shard_map/ppermute | solution.py:39
  167.0 18.0 %all_to_all.17 = bf16[16,48,512]{2,1,0:T(8,128)(2,1)S(1)} all-to-all(bf16[16,48,512]{2,1,0:T(8,128)(2,1)S(1)} %bitcast.134), channel_id=1, replica_groups=mesh['z'=8,'core'=2,'y'=4,'x'=4] {'y','x'}, dimensions={0} | all-to-all | bytes 1572864 | tf_op jit(solution)/shard_map/all_to_all | solution.py:309
  (161 shorter events, 47.1 us)
Async XLA Ops:
  9.7 5.8 %collective-permute-start.5 = (bf16[48,896]{1,0:T(8,128)(2,1)S(1)}, bf16[48,896]{1,0:T(8,128)(2,1)S(1)}, u32[]{:S(2)}, u32[]{:S(2)}) collective-permute-start(bf16[48,896]{1,0:T(8,128)(2,1)S(1)} %slice.330), channel_id=1, source_target_pairs={{0,32},{16,240},{32,64},{48,16},{64,96},{80,48},{96,128},{112,80},... | collective-permute-start | bytes 258056 | tf_op jit(solution)/shard_map/ppermute | solution.py:39
  11.8 6.3 %collective-permute-start.2 = (bf16[2,48,768]{2,1,0:T(8,128)(2,1)S(1)}, bf16[2,48,768]{2,1,0:T(8,128)(2,1)S(1)}, u32[]{:S(2)}, u32[]{:S(2)}) collective-permute-start(bf16[2,48,768]{2,1,0:T(8,128)(2,1)S(1)} %fusion.32), channel_id=1, source_target_pairs={{0,32},{16,240},{32,64},{48,16},{64,96},{80,48},{96,128},{112,80},... | collective-permute-start | bytes 442376 | tf_op jit(solution)/shard_map/ppermute | solution.py:39
  15.6 6.3 %collective-permute-start.6 = (bf16[2,48,896]{2,1,0:T(8,128)(2,1)S(1)}, bf16[2,48,896]{2,1,0:T(8,128)(2,1)S(1)}, u32[]{:S(2)}, u32[]{:S(2)}) collective-permute-start(bf16[2,48,896]{2,1,0:T(8,128)(2,1)S(1)} %fusion.27), channel_id=1, source_target_pairs={{0,32},{16,240},{32,64},{48,16},{64,96},{80,48},{96,128},{112,80},... | collective-permute-start | bytes 516104 | tf_op jit(solution)/shard_map/ppermute | solution.py:39
  18.2 6.4 %collective-permute-start.3 = (bf16[2,48,768]{2,1,0:T(8,128)(2,1)S(1)}, bf16[2,48,768]{2,1,0:T(8,128)(2,1)S(1)}, u32[]{:S(2)}, u32[]{:S(2)}) collective-permute-start(bf16[2,48,768]{2,1,0:T(8,128)(2,1)S(1)} %fusion.33), channel_id=1, source_target_pairs={{0,32},{16,240},{32,64},{48,16},{64,96},{80,48},{96,128},{112,80},... | collective-permute-start | bytes 442376 | tf_op jit(solution)/shard_map/ppermute | solution.py:39
  22.0 6.4 %collective-permute-start.7 = (bf16[2,48,896]{2,1,0:T(8,128)(2,1)S(1)}, bf16[2,48,896]{2,1,0:T(8,128)(2,1)S(1)}, u32[]{:S(2)}, u32[]{:S(2)}) collective-permute-start(bf16[2,48,896]{2,1,0:T(8,128)(2,1)S(1)} %fusion.28), channel_id=1, source_target_pairs={{0,32},{16,240},{32,64},{48,16},{64,96},{80,48},{96,128},{112,80},... | collective-permute-start | bytes 516104 | tf_op jit(solution)/shard_map/ppermute | solution.py:39
  24.7 6.4 %collective-permute-start.4 = (bf16[2,48,768]{2,1,0:T(8,128)(2,1)S(1)}, bf16[2,48,768]{2,1,0:T(8,128)(2,1)S(1)}, u32[]{:S(2)}, u32[]{:S(2)}) collective-permute-start(bf16[2,48,768]{2,1,0:T(8,128)(2,1)S(1)} %fusion.34), channel_id=1, source_target_pairs={{0,32},{16,240},{32,64},{48,16},{64,96},{80,48},{96,128},{112,80},... | collective-permute-start | bytes 442376 | tf_op jit(solution)/shard_map/ppermute | solution.py:39
  28.5 5.5 %collective-permute-start.8 = (bf16[2,48,896]{2,1,0:T(8,128)(2,1)S(1)}, bf16[2,48,896]{2,1,0:T(8,128)(2,1)S(1)}, u32[]{:S(2)}, u32[]{:S(2)}) collective-permute-start(bf16[2,48,896]{2,1,0:T(8,128)(2,1)S(1)} %fusion.29), channel_id=1, source_target_pairs={{0,32},{16,240},{32,64},{48,16},{64,96},{80,48},{96,128},{112,80},... | collective-permute-start | bytes 516104 | tf_op jit(solution)/shard_map/ppermute | solution.py:39
  105.9 5.9 %collective-permute-start.16 = (bf16[48,1024]{1,0:T(8,128)(2,1)S(1)}, bf16[48,1024]{1,0:T(8,128)(2,1)S(1)}, u32[]{:S(2)}, u32[]{:S(2)}) collective-permute-start(bf16[48,1024]{1,0:T(8,128)(2,1)S(1)} %slice.355), channel_id=1, source_target_pairs={{0,32},{16,240},{32,64},{48,16},{64,96},{80,48},{96,128},{112,80},... | collective-permute-start | bytes 294920 | tf_op jit(solution)/shard_map/ppermute | solution.py:39
  108.9 5.8 %collective-permute-start.13 = (bf16[2,48,896]{2,1,0:T(8,128)(2,1)S(1)}, bf16[2,48,896]{2,1,0:T(8,128)(2,1)S(1)}, u32[]{:S(2)}, u32[]{:S(2)}) collective-permute-start(bf16[2,48,896]{2,1,0:T(8,128)(2,1)S(1)} %fusion.24), channel_id=1, source_target_pairs={{0,32},{16,240},{32,64},{48,16},{64,96},{80,48},{96,128},{112,80},... | collective-permute-start | bytes 516104 | tf_op jit(solution)/shard_map/ppermute | solution.py:39
  111.9 6.6 %collective-permute-start.17 = (bf16[2,48,1024]{2,1,0:T(8,128)(2,1)S(1)}, bf16[2,48,1024]{2,1,0:T(8,128)(2,1)S(1)}, u32[]{:S(2)}, u32[]{:S(2)}) collective-permute-start(bf16[2,48,1024]{2,1,0:T(8,128)(2,1)S(1)} %fusion.20), channel_id=1, source_target_pairs={{0,32},{16,240},{32,64},{48,16},{64,96},{80,48},{96,128},{112,80},... | collective-permute-start | bytes 589832 | tf_op jit(solution)/shard_map/ppermute | solution.py:39
  114.8 6.7 %collective-permute-start.14 = (bf16[2,48,896]{2,1,0:T(8,128)(2,1)S(1)}, bf16[2,48,896]{2,1,0:T(8,128)(2,1)S(1)}, u32[]{:S(2)}, u32[]{:S(2)}) collective-permute-start(bf16[2,48,896]{2,1,0:T(8,128)(2,1)S(1)} %fusion.25), channel_id=1, source_target_pairs={{0,32},{16,240},{32,64},{48,16},{64,96},{80,48},{96,128},{112,80},... | collective-permute-start | bytes 516104 | tf_op jit(solution)/shard_map/ppermute | solution.py:39
  118.6 6.7 %collective-permute-start.18 = (bf16[2,48,1024]{2,1,0:T(8,128)(2,1)S(1)}, bf16[2,48,1024]{2,1,0:T(8,128)(2,1)S(1)}, u32[]{:S(2)}, u32[]{:S(2)}) collective-permute-start(bf16[2,48,1024]{2,1,0:T(8,128)(2,1)S(1)} %fusion.21), channel_id=1, source_target_pairs={{0,32},{16,240},{32,64},{48,16},{64,96},{80,48},{96,128},{112,80},... | collective-permute-start | bytes 589832 | tf_op jit(solution)/shard_map/ppermute | solution.py:39
  121.5 6.7 %collective-permute-start.15 = (bf16[2,48,896]{2,1,0:T(8,128)(2,1)S(1)}, bf16[2,48,896]{2,1,0:T(8,128)(2,1)S(1)}, u32[]{:S(2)}, u32[]{:S(2)}) collective-permute-start(bf16[2,48,896]{2,1,0:T(8,128)(2,1)S(1)} %fusion.26), channel_id=1, source_target_pairs={{0,32},{16,240},{32,64},{48,16},{64,96},{80,48},{96,128},{112,80},... | collective-permute-start | bytes 516104 | tf_op jit(solution)/shard_map/ppermute | solution.py:39
  125.3 5.7 %collective-permute-start.19 = (bf16[2,48,1024]{2,1,0:T(8,128)(2,1)S(1)}, bf16[2,48,1024]{2,1,0:T(8,128)(2,1)S(1)}, u32[]{:S(2)}, u32[]{:S(2)}) collective-permute-start(bf16[2,48,1024]{2,1,0:T(8,128)(2,1)S(1)} %fusion.22), channel_id=1, source_target_pairs={{0,32},{16,240},{32,64},{48,16},{64,96},{80,48},{96,128},{112,80},... | collective-permute-start | bytes 589832 | tf_op jit(solution)/shard_map/ppermute | solution.py:39
  134.7 6.5 %collective-permute-start.25 = (bf16[2,48,896]{2,1,0:T(8,128)(2,1)S(1)}, bf16[2,48,896]{2,1,0:T(8,128)(2,1)S(1)}, u32[]{:S(2)}, u32[]{:S(2)}) collective-permute-start(bf16[2,48,896]{2,1,0:T(8,128)(2,1)S(1)} %get-tuple-element.25), channel_id=1, source_target_pairs={{0,32},{16,240},{32,64},{48,16},{64,96},{80,48},{96,128},{112,80},... | collective-permute-start | bytes 516104 | tf_op jit(solution)/shard_map/ppermute | solution.py:39
  138.2 7.1 %collective-permute-start.23 = (bf16[2,48,896]{2,1,0:T(8,128)(2,1)S(1)}, bf16[2,48,896]{2,1,0:T(8,128)(2,1)S(1)}, u32[]{:S(2)}, u32[]{:S(2)}) collective-permute-start(bf16[2,48,896]{2,1,0:T(8,128)(2,1)S(1)} %get-tuple-element.26), channel_id=1, source_target_pairs={{0,32},{16,240},{32,64},{48,16},{64,96},{80,48},{96,128},{112,80},... | collective-permute-start | bytes 516104 | tf_op jit(solution)/shard_map/ppermute | solution.py:39
  141.2 5.5 %collective-permute-start.26 = (bf16[2,48,896]{2,1,0:T(8,128)(2,1)S(1)}, bf16[2,48,896]{2,1,0:T(8,128)(2,1)S(1)}, u32[]{:S(2)}, u32[]{:S(2)}) collective-permute-start(bf16[2,48,896]{2,1,0:T(8,128)(2,1)S(1)} %collective-permute-done.25), channel_id=1, source_target_pairs={{0,16},{16,0},{1,17},{17,1},{2,18},{18,2},{3,19},{19,3},{4,20},{20... | collective-permute-start | bytes 516104 | tf_op jit(solution)/shard_map/ppermute | solution.py:30
  141.6 12.3 %collective-permute-start.29 = (bf16[2,48,896]{2,1,0:T(8,128)(2,1)S(1)}, bf16[2,48,896]{2,1,0:T(8,128)(2,1)S(1)}, u32[]{:S(2)}, u32[]{:S(2)}) collective-permute-start(bf16[2,48,896]{2,1,0:T(8,128)(2,1)S(1)} %collective-permute-done.25), channel_id=1, source_target_pairs={{0,32},{16,240},{32,64},{48,16},{64,96},{80,48},{96,128},{112,80},... | collective-permute-start | bytes 516104 | tf_op jit(solution)/shard_map/ppermute | solution.py:39
  145.3 5.4 %collective-permute-start.27 = (bf16[2,48,896]{2,1,0:T(8,128)(2,1)S(1)}, bf16[2,48,896]{2,1,0:T(8,128)(2,1)S(1)}, u32[]{:S(2)}, u32[]{:S(2)}) collective-permute-start(bf16[2,48,896]{2,1,0:T(8,128)(2,1)S(1)} %collective-permute-done.23), channel_id=1, source_target_pairs={{0,32},{16,240},{32,64},{48,16},{64,96},{80,48},{96,128},{112,80},... | collective-permute-start | bytes 516104 | tf_op jit(solution)/shard_map/ppermute | solution.py:39
  150.7 6.0 %collective-permute-start.31 = (bf16[2,48,896]{2,1,0:T(8,128)(2,1)S(1)}, bf16[2,48,896]{2,1,0:T(8,128)(2,1)S(1)}, u32[]{:S(2)}, u32[]{:S(2)}) collective-permute-start(bf16[2,48,896]{2,1,0:T(8,128)(2,1)S(1)} %collective-permute-done.27), channel_id=1, source_target_pairs={{0,32},{16,240},{32,64},{48,16},{64,96},{80,48},{96,128},{112,80},... | collective-permute-start | bytes 516104 | tf_op jit(solution)/shard_map/ppermute | solution.py:39
  153.8 6.6 %collective-permute-start.33 = (bf16[2,48,896]{2,1,0:T(8,128)(2,1)S(1)}, bf16[2,48,896]{2,1,0:T(8,128)(2,1)S(1)}, u32[]{:S(2)}, u32[]{:S(2)}) collective-permute-start(bf16[2,48,896]{2,1,0:T(8,128)(2,1)S(1)} %collective-permute-done.29), channel_id=1, source_target_pairs={{0,32},{16,240},{32,64},{48,16},{64,96},{80,48},{96,128},{112,80},... | collective-permute-start | bytes 516104 | tf_op jit(solution)/shard_map/ppermute | solution.py:39
  156.7 10.0 %collective-permute-start.35 = (bf16[2,48,896]{2,1,0:T(8,128)(2,1)S(1)}, bf16[2,48,896]{2,1,0:T(8,128)(2,1)S(1)}, u32[]{:S(2)}, u32[]{:S(2)}) collective-permute-start(bf16[2,48,896]{2,1,0:T(8,128)(2,1)S(1)} %collective-permute-done.31), channel_id=1, source_target_pairs={{0,32},{16,240},{32,64},{48,16},{64,96},{80,48},{96,128},{112,80},... | collective-permute-start | bytes 516104 | tf_op jit(solution)/shard_map/ppermute | solution.py:39
  160.4 5.8 %collective-permute-start.32 = (bf16[2,48,896]{2,1,0:T(8,128)(2,1)S(1)}, bf16[2,48,896]{2,1,0:T(8,128)(2,1)S(1)}, u32[]{:S(2)}, u32[]{:S(2)}) collective-permute-start(bf16[2,48,896]{2,1,0:T(8,128)(2,1)S(1)} %collective-permute-done.31), channel_id=1, source_target_pairs={{0,16},{16,0},{1,17},{17,1},{2,18},{18,2},{3,19},{19,3},{4,20},{20... | collective-permute-start | bytes 516104 | tf_op jit(solution)/shard_map/ppermute | solution.py:30
  160.4 5.5 %collective-permute-start.36 = (bf16[2,48,896]{2,1,0:T(8,128)(2,1)S(1)}, bf16[2,48,896]{2,1,0:T(8,128)(2,1)S(1)}, u32[]{:S(2)}, u32[]{:S(2)}) collective-permute-start(bf16[2,48,896]{2,1,0:T(8,128)(2,1)S(1)} %collective-permute-done.33), channel_id=1, source_target_pairs={{0,32},{16,240},{32,64},{48,16},{64,96},{80,48},{96,128},{112,80},... | collective-permute-start | bytes 516104 | tf_op jit(solution)/shard_map/ppermute | solution.py:39
  (22 other events, 164.4 us)
